TPU v7x, 256 devices: a whole 4x4x8 slice. The times are simulated.
256 devices in a mesh: gx: 8 (over y_lo, x), gy: 32 (over z, y_hi, core).
Axes of the slice: x: 4, y: 4 (y_hi: 2, y_lo: 2; y = y_hi * 2 + y_lo), z: 8, core: 2. Of those that a mesh axis runs over, the one named last changes fastest.
Arguments:
- beam_states: bfloat16 [128, 16384], P('gy', 'gx'), may hold values from -6 to 6
- step_tokens: bfloat16 [2, 128, 16384], P(None, 'gy', 'gx'), may hold values from -6 to 6
- norm_gain: bfloat16 [16384], P('gx'), may hold values from 0.25 to 1.75
- w_gate: bfloat16 [16384, 28672], P('gx', 'gy'), may hold values from -0.046875 to 0.046875
- w_up: bfloat16 [16384, 28672], P('gx', 'gy'), may hold values from -0.046875 to 0.046875
- w_down: bfloat16 [28672, 16384], P('gy', 'gx'), may hold values from -0.03125 to 0.03125
- prompt_table: bfloat16 [256, 16384], P(None, 'gx'), may hold values from -6 to 6
- kept_beams: int32 [8], replicated, may hold values from 0 to 127, as said below
- prompt_ids: int32 [8, 16], replicated, may hold values from 0 to 255
Outputs:
- decoded: bfloat16 [128, 16384], P('gy', 'gx')
- evaluated: bfloat16 [128, 16384], P('gy', 'gx')
Inputs may be any that keep to these rules, and one draw needn't show every extreme that they name: `kept_beams`: distinct beam indices.
All inputs are finite; a program needn't handle non-finite values.
Results may differ from a plain program's by a relative error of at most 0.014.
Values may be sent and summed in bfloat16 or wider, within the bound.
A program may use at most 64 MiB of HBM per device.

v0:
```python
import jax
import jax.numpy as jnp
from jax import lax
from jax.sharding import PartitionSpec as P

D = 16384
STEPS = 2


EPS = 1e-05


def cut_along(array, dim, peers):
    before, after = (array.shape[:dim], array.shape[dim + 1 :])
    return jnp.moveaxis(array.reshape(*before, peers, -1, *after), dim, 0)


def sent_and_summed(array, axis, dim):
    peers = lax.axis_size(axis)
    pieces = lax.all_to_all(cut_along(array, dim, peers), axis, 0, 0, tiled=True)
    return jnp.sum(pieces.astype(jnp.float32), axis=0)


def side_by_side(arrays, axis, dim, along):
    columns = [a.reshape(*a.shape[:along], -1) for a in arrays]
    both = jnp.concatenate(columns, axis=along)
    whole, at, done = (sent_and_summed(both, axis, dim), 0, [])
    for a, column in zip(arrays, columns):
        share = whole[..., at : at + column.shape[along]]
        done.append(share.reshape(*share.shape[:along], *a.shape[along:]))
        at += column.shape[along]
    return tuple(done)


def in_order(pieces, dim):
    dims = list(pieces.shape[1:])
    dims[dim] *= pieces.shape[0]
    return jnp.moveaxis(pieces, 0, dim).reshape(dims)


def from_everyone(array, axis):
    copies = jnp.broadcast_to(array, (lax.axis_size(axis), *array.shape))
    return lax.all_to_all(copies, axis, split_axis=0, concat_axis=0, tiled=True)


def gathered_copies(array, axis, dim):
    return in_order(from_everyone(array, axis), dim)


def activate(gate_part, upper_part, squares):
    scale = lax.rsqrt(squares / D + EPS)[:, None]
    return (jax.nn.silu(scale * gate_part) * (scale * upper_part)).astype(jnp.bfloat16)


def on_device(
    beam_states, step_tokens, norm_gain, w_gate, w_up, w_down, prompt_table, kept_beams, prompt_ids
):
    gain = norm_gain.astype(jnp.float32)

    def layer_rows(rows):
        values = rows.astype(jnp.float32)
        squares = jnp.sum(values * values, axis=1)
        scaled = (values * gain).astype(jnp.bfloat16)
        gate_part = jnp.dot(scaled, w_gate, preferred_element_type=jnp.float32)
        upper_part = jnp.dot(scaled, w_up, preferred_element_type=jnp.float32)
        gate_sum, upper_sum, square_sum = side_by_side(
            (
                gate_part.astype(jnp.bfloat16),
                upper_part.astype(jnp.bfloat16),
                squares.astype(jnp.bfloat16),
            ),
            "gx",
            0,
            1,
        )
        hidden = gathered_copies(activate(gate_sum, upper_sum, square_sum), "gx", 0)
        return sent_and_summed(
            jnp.dot(hidden, w_down, preferred_element_type=jnp.float32).astype(jnp.bfloat16),
            "gy",
            0,
        )

    state = beam_states
    for step in range(STEPS):
        mixed = (state.astype(jnp.float32) + step_tokens[step].astype(jnp.float32)).astype(
            jnp.bfloat16
        )
        gathered = gathered_copies(mixed, "gy", 0)
        state = (mixed.astype(jnp.float32) + layer_rows(gathered)).astype(jnp.bfloat16)
    every_beam = gathered_copies(state, "gy", 0)
    beam_index = lax.iota(jnp.int32, every_beam.shape[0])
    picker = (kept_beams[:, None] == beam_index[None, :]).astype(jnp.bfloat16)
    chosen = jnp.dot(picker, every_beam, preferred_element_type=jnp.float32)
    flat_ids = prompt_ids.reshape(-1)
    token_index = lax.iota(jnp.int32, prompt_table.shape[0])
    lookup = (flat_ids[:, None] == token_index[None, :]).astype(jnp.bfloat16)
    words = jnp.dot(lookup, prompt_table, preferred_element_type=jnp.float32)
    rows = (jnp.repeat(chosen, prompt_ids.shape[1], axis=0) + words).astype(jnp.bfloat16)
    share = rows.shape[0] // lax.axis_size("gy")
    own_rows = lax.dynamic_slice_in_dim(rows, lax.axis_index("gy") * share, share, 0)
    evaluated = (own_rows.astype(jnp.float32) + layer_rows(rows)).astype(jnp.bfloat16)
    return (state, evaluated)


def solution(mesh):
    return jax.shard_map(
        on_device,
        mesh=mesh,
        in_specs=(
            P("gy", "gx"),
            P(None, "gy", "gx"),
            P("gx"),
            P("gx", "gy"),
            P("gx", "gy"),
            P("gy", "gx"),
            P(None, "gx"),
            P(),
            P(),
        ),
        out_specs=(P("gy", "gx"), P("gy", "gx")),
        check_vma=False,
    )
```

profile of v0, /device:TPU:1, one launch (start us, length us, event | category | flops | bytes accessed | tf_op | source)
XLA Modules:
  0.0 238.4 jit_solution(7009970679203027732)
XLA Ops:
  0.6 0.0 copy-start
  0.6 0.8 fusion.13
  1.5 1.0 broadcast_in_dim.14
  2.5 12.8 %all-to-all-start = ((bf16[32,4,2048]{2,1,0:T(4,128)(2,1)}), bf16[32,4,2048]{2,1,0:T(4,128)(2,1)S(1)}, u32[]{:S(2)}, u32[]{:S(2)}) async-start(bf16[32,4,2048]{2,1,0:T(4,128)(2,1)} %broadcast_in_dim.14), calls=%async_computation | async-start | bytes 1048576 | tf_op jit(solution)/shard_map/all_to_all | solution.py:43
  15.3 0.7 convert_element_type.183
  16.0 16.3 %all-to-all-done = bf16[32,4,2048]{2,1,0:T(4,128)(2,1)S(1)} async-done(((bf16[32,4,2048]{2,1,0:T(4,128)(2,1)}), bf16[32,4,2048]{2,1,0:T(4,128)(2,1)S(1)}, u32[]{:S(2)}, u32[]{:S(2)}) %all-to-all-start) | async-done | bytes 524320 | tf_op jit(solution)/shard_map/all_to_all | solution.py:43
  32.3 0.4 multiply_reduce_fusion.1
  32.6 0.1 convert_element_type.230
  32.7 0.1 reshape.108
  32.8 0.0 copy-start.2
  32.8 2.9 %convolution_convert_fusion.7 = bf16[128,896]{1,0:T(8,128)(2,1)S(1)} fusion(bf16[2048,896]{1,0:T(8,128)(2,1)} %param.13, f32[128,2048]{1,0:T(8,128)S(1)} %reshape.108, f32[2048]{0:T(1024)S(1)} %convert_element_type.183), kind=kOutput, calls=%fused_computation.11 | convolution fusion | flops 470401024 | bytes 4956160 | tf_op jit(solution)/shard_map/dot_general | solution.py:65
  35.7 0.2 copy-done.2
  36.0 0.7 convolution_convert_fusion.8
  36.8 12.5 %all_to_all.60 = bf16[8,16,1793]{2,1,0:T(8,128)(2,1)S(1)} all-to-all(bf16[8,16,1793]{2,1,0:T(8,128)(2,1)S(1)} %pad_maximum_fusion), channel_id=1, replica_groups=mesh['gx'=8,'gy'=32] {'gx'}, dimensions={0} | all-to-all | bytes 918016 | tf_op jit(solution)/shard_map/all_to_all | solution.py:20
  49.2 0.1 convert_reduce_fusion.5
  49.3 0.1 fusion.22
  49.4 0.1 fusion.11
  49.6 8.4 %all_to_all.61 = bf16[8,16,896]{2,1,0:T(8,128)(2,1)S(1)} all-to-all(bf16[8,16,896]{2,1,0:T(8,128)(2,1)S(1)} %broadcast_in_dim.15), channel_id=1, replica_groups=mesh['gx'=8,'gy'=32] {'gx'}, dimensions={0} | all-to-all | bytes 458752 | tf_op jit(solution)/shard_map/all_to_all | solution.py:43
  58.0 0.7 convolution_convert_fusion.2
  58.7 0.2 reshape.100
  58.9 25.8 %all_to_all.62 = bf16[32,4,2048]{2,1,0:T(4,128)(2,1)S(1)} all-to-all(bf16[32,4,2048]{2,1,0:T(4,128)(2,1)S(1)} %reshape.100), channel_id=1, replica_groups=mesh['gx'=8,'gy'=32] {'gy'}, dimensions={0} | all-to-all | bytes 1048576 | tf_op jit(solution)/shard_map/all_to_all | solution.py:20
  84.7 0.2 convert_reduce_fusion.2
  85.0 0.2 broadcast_in_dim.32
  85.2 22.5 %all_to_all.63 = bf16[32,4,2048]{2,1,0:T(4,128)(2,1)S(1)} all-to-all(bf16[32,4,2048]{2,1,0:T(4,128)(2,1)S(1)} %broadcast_in_dim.32), channel_id=1, replica_groups=mesh['gx'=8,'gy'=32] {'gy'}, dimensions={0} | all-to-all | bytes 1048576 | tf_op jit(solution)/shard_map/all_to_all | solution.py:43
  107.7 0.1 reshape.110
  107.8 2.9 %convolution_convert_fusion.5 = bf16[128,896]{1,0:T(8,128)(2,1)S(1)} fusion(bf16[2048,896]{1,0:T(8,128)(2,1)} %param.13, f32[128,2048]{1,0:T(8,128)S(1)} %reshape.110, f32[2048]{0:T(1024)S(1)} %convert_element_type.183), kind=kOutput, calls=%fused_computation.9 | convolution fusion | flops 470401024 | bytes 4956160 | tf_op jit(solution)/shard_map/dot_general | solution.py:65
  110.7 0.2 copy-done.3
  110.9 0.8 convolution_convert_fusion.6
  111.7 0.4 multiply_reduce_fusion
  112.0 0.1 convert_element_type.231
  112.2 11.0 %all_to_all.64 = bf16[8,16,1793]{2,1,0:T(8,128)(2,1)S(1)} all-to-all(bf16[8,16,1793]{2,1,0:T(8,128)(2,1)S(1)} %pad_maximum_fusion.1), channel_id=1, replica_groups=mesh['gx'=8,'gy'=32] {'gx'}, dimensions={0} | all-to-all | bytes 918016 | tf_op jit(solution)/shard_map/all_to_all | solution.py:20
  123.2 0.1 convert_reduce_fusion.4
  123.3 0.1 fusion.19
  123.4 0.1 fusion.9
  123.5 8.5 %all_to_all.65 = bf16[8,16,896]{2,1,0:T(8,128)(2,1)S(1)} all-to-all(bf16[8,16,896]{2,1,0:T(8,128)(2,1)S(1)} %broadcast_in_dim.33), channel_id=1, replica_groups=mesh['gx'=8,'gy'=32] {'gx'}, dimensions={0} | all-to-all | bytes 458752 | tf_op jit(solution)/shard_map/all_to_all | solution.py:43
  132.0 2.8 %convolution_convert_fusion.1 = bf16[128,2048]{1,0:T(8,128)(2,1)S(1)} fusion(bf16[128,896]{1,0:T(8,128)(2,1)S(1)} %bitcast.32, bf16[896,2048]{1,0:T(8,128)(2,1)} %param.14), kind=kOutput, calls=%fused_computation.2 | convolution fusion | flops 470024192 | bytes 4423680 | tf_op jit(solution)/shard_map/dot_general | solution.py:78
  134.8 0.2 reshape.102
  135.0 25.0 %all_to_all.66 = bf16[32,4,2048]{2,1,0:T(4,128)(2,1)S(1)} all-to-all(bf16[32,4,2048]{2,1,0:T(4,128)(2,1)S(1)} %reshape.102), channel_id=1, replica_groups=mesh['gx'=8,'gy'=32] {'gy'}, dimensions={0} | all-to-all | bytes 1048576 | tf_op jit(solution)/shard_map/all_to_all | solution.py:20
  160.0 0.2 convert_reduce_fusion.1
  160.2 0.0 copy-start.6
  160.3 1.0 broadcast_in_dim.34
  161.3 5.7 %all-to-all-start.8 = ((bf16[32,4,2048]{2,1,0:T(4,128)(2,1)}), bf16[32,4,2048]{2,1,0:T(4,128)(2,1)S(1)}, u32[]{:S(2)}, u32[]{:S(2)}) async-start(bf16[32,4,2048]{2,1,0:T(4,128)(2,1)} %broadcast_in_dim.34), calls=%async_computation.8 | async-start | bytes 1048576 | tf_op jit(solution)/shard_map/all_to_all | solution.py:43
  167.0 0.1 eq.31
  167.1 16.9 %all-to-all-done.8 = bf16[32,4,2048]{2,1,0:T(4,128)(2,1)S(1)} async-done(((bf16[32,4,2048]{2,1,0:T(4,128)(2,1)}), bf16[32,4,2048]{2,1,0:T(4,128)(2,1)S(1)}, u32[]{:S(2)}, u32[]{:S(2)}) %all-to-all-start.8) | async-done | bytes 524320 | tf_op jit(solution)/shard_map/all_to_all | solution.py:43
  184.0 0.1 reshape.103
  184.1 0.2 fusion.23
  184.4 0.1 broadcast_in_dim.35
  184.5 0.4 fusion.2
  184.9 1.2 copy-done.1
  186.2 0.7 convolution_convert_fusion.3
  186.9 0.5 copy-done.4
  187.4 0.7 convolution_convert_fusion.4
  188.1 0.2 convert_element_type.232
  188.4 11.0 %all_to_all.67 = bf16[8,16,1793]{2,1,0:T(8,128)(2,1)S(1)} all-to-all(bf16[8,16,1793]{2,1,0:T(8,128)(2,1)S(1)} %pad_maximum_fusion.2), channel_id=1, replica_groups=mesh['gx'=8,'gy'=32] {'gx'}, dimensions={0} | all-to-all | bytes 918016 | tf_op jit(solution)/shard_map/all_to_all | solution.py:20
  199.4 0.1 convert_reduce_fusion.3
  199.4 0.1 fusion.16
  199.6 0.1 fusion.7
  199.7 8.5 %all_to_all.68 = bf16[8,16,896]{2,1,0:T(8,128)(2,1)S(1)} all-to-all(bf16[8,16,896]{2,1,0:T(8,128)(2,1)S(1)} %broadcast_in_dim.36), channel_id=1, replica_groups=mesh['gx'=8,'gy'=32] {'gx'}, dimensions={0} | all-to-all | bytes 458752 | tf_op jit(solution)/shard_map/all_to_all | solution.py:43
  208.2 2.8 %convolution_convert_fusion = bf16[128,2048]{1,0:T(8,128)(2,1)S(1)} fusion(bf16[128,896]{1,0:T(8,128)(2,1)S(1)} %bitcast.33, bf16[896,2048]{1,0:T(8,128)(2,1)} %param.14), kind=kOutput, calls=%fused_computation.1 | convolution fusion | flops 470024192 | bytes 4423680 | tf_op jit(solution)/shard_map/dot_general | solution.py:78
  211.0 1.0 reshape.106
  212.0 8.6 %all-to-all-start.11 = ((bf16[32,4,2048]{2,1,0:T(4,128)(2,1)}), bf16[32,4,2048]{2,1,0:T(4,128)(2,1)S(1)}, u32[]{:S(2)}, u32[]{:S(2)}) async-start(bf16[32,4,2048]{2,1,0:T(4,128)(2,1)} %reshape.106), calls=%async_computation.11 | async-start | bytes 1048576 | tf_op jit(solution)/shard_map/all_to_all | solution.py:20
  220.6 17.0 %all-to-all-done.11 = bf16[32,4,2048]{2,1,0:T(4,128)(2,1)S(1)} async-done(((bf16[32,4,2048]{2,1,0:T(4,128)(2,1)}), bf16[32,4,2048]{2,1,0:T(4,128)(2,1)S(1)}, u32[]{:S(2)}, u32[]{:S(2)}) %all-to-all-start.11) | async-done | bytes 524320 | tf_op jit(solution)/shard_map/all_to_all | solution.py:20
  237.6 0.2 convert_reduce_fusion
  237.8 0.6 add_convert_fusion
  (21 shorter events, 0.2 us)
Async XLA Ops:
  0.6 183.9 %copy-start = (bf16[256,2048]{1,0:T(8,128)(2,1)S(1)}, bf16[256,2048]{1,0:T(8,128)(2,1)}, u32[]{:S(2)}) copy-start(bf16[256,2048]{1,0:T(8,128)(2,1)} %param.15) | copy-start | bytes 3145732
  2.5 29.8 %all-to-all-start = ((bf16[32,4,2048]{2,1,0:T(4,128)(2,1)}), bf16[32,4,2048]{2,1,0:T(4,128)(2,1)S(1)}, u32[]{:S(2)}, u32[]{:S(2)}) async-start(bf16[32,4,2048]{2,1,0:T(4,128)(2,1)} %broadcast_in_dim.14), calls=%async_computation | async-start | bytes 1048576 | tf_op jit(solution)/shard_map/all_to_all | solution.py:43
  32.8 3.1 %copy-start.2 = (bf16[2048,896]{1,0:T(8,128)(2,1)S(1)}, bf16[2048,896]{1,0:T(8,128)(2,1)}, u32[]{:S(2)}) copy-start(bf16[2048,896]{1,0:T(8,128)(2,1)} %param.12) | copy-start | bytes 11010052
  36.0 22.1 %copy-start.5 = (bf16[896,2048]{1,0:T(8,128)(2,1)S(1)}, bf16[896,2048]{1,0:T(8,128)(2,1)}, u32[]{:S(2)}) copy-start(bf16[896,2048]{1,0:T(8,128)(2,1)} %param.14) | copy-start | bytes 11010052
  49.6 35.4 %copy-start.7 = (bf16[2,4,2048]{2,1,0:T(4,128)(2,1)S(1)}, bf16[2,4,2048]{2,1,0:T(4,128)(2,1)}, u32[]{:S(2)}) copy-start(bf16[2,4,2048]{2,1,0:T(4,128)(2,1)} %param.10) | copy-start | bytes 98308
  107.8 3.1 %copy-start.3 = (bf16[2048,896]{1,0:T(8,128)(2,1)S(1)}, bf16[2048,896]{1,0:T(8,128)(2,1)}, u32[]{:S(2)}) copy-start(bf16[2048,896]{1,0:T(8,128)(2,1)} %param.12) | copy-start | bytes 11010052
  132.0 35.0 %copy-start.8 = (s32[8,16]{1,0:T(8,128)S(1)}, s32[8,16]{1,0:T(8,128)}, u32[]{:S(2)}) copy-start(s32[8,16]{1,0:T(8,128)} %param.17) | copy-start | bytes 1540
  134.8 49.3 %copy-start.9 = (s32[8]{0:T(128)S(1)}, s32[8]{0:T(128)}, u32[]{:S(2)}) copy-start(s32[8]{0:T(128)} %param.16) | copy-start | bytes 100
  160.2 26.7 %copy-start.6 = (bf16[4,2048]{1,0:T(4,128)(2,1)}, bf16[4,2048]{1,0:T(4,128)(2,1)S(1)}, u32[]{:S(2)}) copy-start(bf16[4,2048]{1,0:T(4,128)(2,1)S(1)} %add_convert_fusion.1) | copy-start | bytes 49156
  161.3 22.7 %all-to-all-start.8 = ((bf16[32,4,2048]{2,1,0:T(4,128)(2,1)}), bf16[32,4,2048]{2,1,0:T(4,128)(2,1)S(1)}, u32[]{:S(2)}, u32[]{:S(2)}) async-start(bf16[32,4,2048]{2,1,0:T(4,128)(2,1)} %broadcast_in_dim.34), calls=%async_computation.8 | async-start | bytes 1048576 | tf_op jit(solution)/shard_map/all_to_all | solution.py:43
  184.1 2.0 copy-start.1
  184.5 2.9 %copy-start.4 = (bf16[2048,896]{1,0:T(8,128)(2,1)S(1)}, bf16[2048,896]{1,0:T(8,128)(2,1)}, u32[]{:S(2)}) copy-start(bf16[2048,896]{1,0:T(8,128)(2,1)} %param.12) | copy-start | bytes 11010052
  212.0 25.6 %all-to-all-start.11 = ((bf16[32,4,2048]{2,1,0:T(4,128)(2,1)}), bf16[32,4,2048]{2,1,0:T(4,128)(2,1)S(1)}, u32[]{:S(2)}, u32[]{:S(2)}) async-start(bf16[32,4,2048]{2,1,0:T(4,128)(2,1)} %reshape.106), calls=%async_computation.11 | async-start | bytes 1048576 | tf_op jit(solution)/shard_map/all_to_all | solution.py:20
where the time goes:
time: 239 us; the launch traced here: 238 us
  blocking collectives  133 us (56%)
  waiting for transfers between devices  50.2 us (21%)
  starting transfers between devices  27 us (11%)
  matrix products  15.8 us (7%)
  local copies, waits for them, and re-layouts  6.73 us (3%)
  other arithmetic  4.57 us (2%)
    all_to_all x5, blocking collectives, sent_and_summed(): lax.all_to_all(cut_along(array, dim, peers), axis, 0, 0, tiled=True)  85.3 us
    all_to_all x4, blocking collectives, from_everyone(): return lax.all_to_all(copies, axis, split_axis=0, concat_axis=0, tiled=True)  47.9 us
    all_to_all x2, waiting for transfers between devices, from_everyone(): return lax.all_to_all(copies, axis, split_axis=0, concat_axis=0, tiled=True)  33.2 us
    all_to_all x2, starting transfers between devices, from_everyone(): return lax.all_to_all(copies, axis, split_axis=0, concat_axis=0, tiled=True)  18.4 us
    all_to_all x1, waiting for transfers between devices, sent_and_summed(): lax.all_to_all(cut_along(array, dim, peers), axis, 0, 0, tiled=True)  17 us
    all_to_all x1, starting transfers between devices, sent_and_summed(): lax.all_to_all(cut_along(array, dim, peers), axis, 0, 0, tiled=True)  8.61 us
    dot_general x3, matrix products, layer_rows(): upper_part = jnp.dot(scaled, w_up, preferred_element_type=jnp.float32)  6.56 us
    dot_general x3, matrix products, layer_rows(): jnp.dot(hidden, w_down, preferred_element_type=jnp.float32)  6.3 us
  transfers between devices with their start and end apart: 3, of which 3 were waited for; matrix products, arithmetic and copies ran while one was open for 0% of the time, Pallas kernels for 0%

commit v1 on v0

v1 whole, which is shorter than its diff:
```python
import functools

import jax
import jax.numpy as jnp
from jax import lax
from jax.experimental import pallas as pl
from jax.experimental.pallas import tpu as pltpu
from jax.sharding import PartitionSpec as P

D = 16384
EPS = 1e-05
BF, F32 = jnp.bfloat16, jnp.float32
NX, NY = 4, 2
NQ = 16
WIDTH = 2048
HID = 896
LAYERS, CHUNKS = 3, 2
MESH = pl.DeviceIdType.MESH

CHIP_STEPS = sorted(range(1, NQ), key=lambda d: -(min(d // 2, 8 - d // 2) + 2 * (d % 2)))
GX_STEPS = sorted(range(1, 8), key=lambda e: -(min(e % 4, 4 - e % 4) + e // 4))


def halves(a, b):
    top = lax.broadcasted_iota(jnp.int32, a.shape, 0) < 4
    return jnp.where(top, a, pltpu.roll(b, 4, 0)), jnp.where(top, pltpu.roll(a, 4, 0), b)


def kernel(
    beam, tok, gain, kept, ids, wg_hbm, wu_hbm, wd_hbm, tab_hbm,
    dec_out, ev_out,
    wg, wu, wd, tab, words, first, x, xs, part, part_in, hid, hid_mm,
    own, sib_out, sib_in, sums, sums_in, tok_out, tok_in,
    pick, pick_sib, pick_all, rows_f, dec_send, dec_in, last, last_in,
    load_sem, snd, first_sem, first_fwd, tok_sem, ag_sem, ag_fwd, rsx_sem, agx_sem,
    sib_sem, rsy_sem, pick_sem, pick_sib_sem, dec_sem, last_sem,
):
    gx, gy = lax.axis_index("gx"), lax.axis_index("gy")
    px, pyl = lax.rem(gx, NX), gx // NX
    core, chip = lax.rem(gy, 2), gy // 2
    yh, z = lax.rem(chip, 2), chip // 2
    other = 1 - core
    sibling = (gx, chip * 2 + other)

    def chip_at(d):
        return lax.rem(z + d // 2, 8) * 2 + lax.rem(yh + d % 2, 2)

    def chip_from(d):
        return lax.rem(z + 8 - d // 2, 8) * 2 + lax.rem(yh + d % 2, 2)

    def gx_at(e):
        return lax.rem(pyl + e // 4, NY) * NX + lax.rem(px + e % 4, NX)

    def gx_from(e):
        return lax.rem(pyl + e // 4, NY) * NX + lax.rem(px + 4 - e % 4, NX)

    def to_chip(q):
        return (gx, q * 2 + core)

    def to_gx(p):
        return (p, gy)

    def remote(src, dst, send, recv, device):
        return pltpu.make_async_remote_copy(
            src_ref=src, dst_ref=dst, send_sem=send, recv_sem=recv, device_id=device, device_id_type=MESH
        )

    sent = []

    loads = [
        pltpu.make_async_copy(s, d, load_sem.at[i])
        for i, (s, d) in enumerate([(tab_hbm, tab), (wg_hbm, wg), (wu_hbm, wu), (wd_hbm, wd)])
    ]
    for load in loads:
        load.start()

    barrier = pltpu.get_barrier_semaphore()
    for d in range(1, NQ):
        pl.semaphore_signal(barrier, inc=1, device_id=to_chip(chip_at(d)), device_id_type=MESH)
    for e in range(1, 8):
        pl.semaphore_signal(barrier, inc=1, device_id=to_gx(gx_at(e)), device_id_type=MESH)
    pl.semaphore_signal(barrier, inc=1, device_id=sibling, device_id_type=MESH)

    mixed = (beam[...].astype(F32) + tok[0].astype(F32)).astype(BF).astype(F32)
    first[core, chip] = jnp.concatenate([mixed[:, :1024], mixed[:, 1024:]], axis=0).astype(BF)
    token = tok[1].astype(F32)
    token = jnp.concatenate([token, token], axis=0).astype(BF)
    for cb in range(NQ):
        tok_out[cb] = token[:, cb * 128 : cb * 128 + 128]

    pl.semaphore_wait(barrier, NQ - 1 + 7 + 1)

    for d in CHIP_STEPS:
        remote(first.at[core, chip], first.at[core, chip], snd.at[0], first_sem.at[d], to_chip(chip_at(d))).start()
    remote(first.at[core, chip], first.at[core, chip], snd.at[1], first_fwd.at[0], sibling).start()
    for d in CHIP_STEPS:
        remote(tok_out.at[chip_at(d)], tok_in.at[chip], snd.at[2], tok_sem.at[d], to_chip(chip_at(d))).start()
    sent.append((first.at[0, pl.ds(0, NQ - 1)], snd.at[0]))
    sent.append((first.at[0], snd.at[1]))
    sent.append((tok_in.at[pl.ds(0, NQ - 1)], snd.at[2]))
    tok_in[chip] = tok_out[chip]

    loads[0].wait()
    lookup = (ids[...] == lax.broadcasted_iota(jnp.int32, (128, 256), 1)).astype(F32).astype(BF)
    for n in range(4):
        cols = slice(n * 512, n * 512 + 512)
        words[:, cols] = jnp.dot(lookup, tab[:, cols], preferred_element_type=F32).astype(BF)

    for d in reversed(CHIP_STEPS):
        q = chip_from(d)
        piece = first.at[core, q]
        remote(piece, piece, snd.at[0], first_sem.at[d], to_chip(chip_at(d))).wait_recv()
        remote(piece, piece, snd.at[1], first_fwd.at[0], sibling).start()
    remote(first.at[other], first.at[other], snd.at[1], first_fwd.at[0], sibling).wait_recv()
    for load in loads[1:3]:
        load.wait()

    def prepare(layer, k):
        squares = []
        for h in range(2):
            total = jnp.zeros((32, 128), F32)
            for cb in range(NQ):
                v = x[layer, k, h, cb].astype(F32)
                total = total + v * v
                cols = slice(cb * 128, cb * 128 + 128)
                xs[h * 32 : h * 32 + 32, cols] = (v * gain[:, cols].astype(F32)).astype(BF)
            squares.append(jnp.sum(total, axis=1, keepdims=True))
        whole = jnp.broadcast_to(jnp.concatenate(squares, axis=0), (64, 128))
        high = whole.astype(BF).astype(F32)
        both = jnp.concatenate([high.reshape(8, 8, 128), (whole - high).reshape(8, 8, 128)], axis=1)
        part[layer, k, :, :, HID:1024] = both.astype(BF)

    def up(layer, k):
        rows = xs[...]

        def tile(n, carry):
            cols = pl.ds(pl.multiple_of(n * 128, 128), 128)
            weights = jnp.concatenate([wg[:, cols], wu[:, cols]], axis=1)
            y = jnp.dot(rows, weights, preferred_element_type=F32)
            both = jnp.concatenate([y[:, :128].reshape(8, 8, 128), y[:, 128:].reshape(8, 8, 128)], axis=1)
            part[layer, k, :, :, cols] = both.astype(BF)
            return carry

        lax.fori_loop(0, HID // 128, tile, 0)
        i = layer * CHUNKS + k
        for e in GX_STEPS:
            p = gx_at(e)
            remote(part.at[layer, k, p], part_in.at[layer, k, e], snd.at[10 + i], rsx_sem.at[i], to_gx(p)).start()
        sent.append((part_in.at[layer, k, pl.ds(1, 7)], snd.at[10 + i]))

    def act(layer, k):
        i = layer * CHUNKS + k
        arrived = part_in.at[layer, k, pl.ds(1, 7)]
        remote(arrived, arrived, snd.at[10 + i], rsx_sem.at[i], to_gx(gx)).wait_recv()
        total = part[layer, k, gx].astype(F32)
        for e in range(1, 8):
            total = total + part_in[layer, k, e].astype(F32)
        squares = total[0:8, HID:1024] + total[8:16, HID:1024]
        scale = lax.rsqrt(squares / D + EPS)
        for n in range(HID // 128):
            cols = slice(n * 128, n * 128 + 128)
            g = scale * total[0:8, cols]
            u = scale * total[8:16, cols]
            hid[layer, k, gx, :, cols] = (g / (1.0 + jnp.exp(-g)) * u).astype(BF)
        piece = hid.at[layer, k, gx]
        for e in GX_STEPS:
            remote(piece, piece, snd.at[20 + i], agx_sem.at[i, e], to_gx(gx_at(e))).start()
        sent.append((hid.at[layer, k, pl.ds(0, 7)], snd.at[20 + i]))

    def down(layer, k):
        i = layer * CHUNKS + k
        for e in reversed(GX_STEPS):
            piece = hid.at[layer, k, gx_from(e)]
            remote(piece, piece, snd.at[20 + i], agx_sem.at[i, e], to_gx(gx)).wait_recv()
        hid_mm[...] = hid[layer, k].astype(F32).reshape(64, HID).astype(BF)
        rows = hid_mm[...]

        def tile(n, carry):
            cols = pl.ds(pl.multiple_of(n * 256, 128), 256)
            y = jnp.dot(rows, wd[:, cols], preferred_element_type=F32)
            mine = jnp.where(core == 0, y[0:32], y[32:64])
            theirs = jnp.where(core == 0, y[32:64], y[0:32]).astype(BF)
            for m in range(2):
                own[k, 2 * n + m] = mine[:, m * 128 : m * 128 + 128]
                sib_out[layer, k, 2 * n + m] = theirs[:, m * 128 : m * 128 + 128]
            return carry

        lax.fori_loop(0, 8, tile, 0)
        remote(sib_out.at[layer, k], sib_in.at[layer, k], snd.at[30 + i], sib_sem.at[i], sibling).start()
        sent.append((sib_out.at[layer, k], snd.at[30 + i]))

    def scatter(layer, k):
        i = layer * CHUNKS + k
        remote(sib_in.at[layer, k], sib_in.at[layer, k], snd.at[30 + i], sib_sem.at[i], sibling).wait_recv()
        for cb in range(NQ):
            sums[layer, k, cb] = (own[k, cb] + sib_in[layer, k, cb].astype(F32)).astype(BF)
        for d in CHIP_STEPS:
            q = chip_at(d)
            remote(sums.at[layer, k, q], sums_in.at[layer, k, d], snd.at[40 + i], rsy_sem.at[i], to_chip(q)).start()
        sent.append((sums_in.at[layer, k, pl.ds(1, NQ - 1)], snd.at[40 + i]))

    def new_state(layer, k):
        i = layer * CHUNKS + k
        arrived = sums_in.at[layer, k, pl.ds(1, NQ - 1)]
        remote(arrived, arrived, snd.at[40 + i], rsy_sem.at[i], sibling).wait_recv()
        total = sums[layer, k, chip].astype(F32)
        for d in range(1, NQ):
            total = total + sums_in[layer, k, d].astype(F32)
        return (x[layer, k, core, chip].astype(F32) + total).astype(BF).astype(F32)

    def spread(k):
        state = new_state(0, k)
        if k == 0:
            for d in CHIP_STEPS:
                piece = tok_in.at[chip_from(d)]
                remote(piece, piece, snd.at[2], tok_sem.at[d], sibling).wait_recv()
        groups = []
        for g in range(4):
            a, b = tok_in[8 * k + 2 * g].astype(F32), tok_in[8 * k + 2 * g + 1].astype(F32)
            groups.append(jnp.where(lax.broadcasted_iota(jnp.int32, (8, 128), 0) < 4, a, b))
        x[1, k, core, chip] = (state + jnp.concatenate(groups, axis=0)).astype(BF)
        piece = x.at[1, k, core, chip]
        for d in CHIP_STEPS:
            remote(piece, piece, snd.at[3 + k], ag_sem.at[k, d], to_chip(chip_at(d))).start()
        remote(piece, piece, snd.at[5 + k], ag_fwd.at[k], sibling).start()
        sent.append((x.at[1, k, 0, pl.ds(0, NQ - 1)], snd.at[3 + k]))
        sent.append((x.at[1, k, 0], snd.at[5 + k]))

    def collect(k):
        for d in reversed(CHIP_STEPS):
            piece = x.at[1, k, core, chip_from(d)]
            remote(piece, piece, snd.at[3 + k], ag_sem.at[k, d], sibling).wait_recv()
            remote(piece, piece, snd.at[5 + k], ag_fwd.at[k], sibling).start()
        theirs = x.at[1, k, other]
        remote(theirs, theirs, snd.at[5 + k], ag_fwd.at[k], sibling).wait_recv()

    for k in range(CHUNKS):
        for h in range(2):
            for g in range(4):
                a, b = first[h, 8 * k + 2 * g].astype(F32), first[h, 8 * k + 2 * g + 1].astype(F32)
                low, high = halves(a, b)
                rows_f[h, 4 * k + g, :, 0:1024] = low
                rows_f[h, 4 * k + g, :, 1024:2048] = high
            for cb in range(NQ):
                block = rows_f[h, 4 * k : 4 * k + 4, :, cb * 128 : cb * 128 + 128]
                x[0, k, h, cb] = block.reshape(32, 128).astype(BF)
        prepare(0, k)
        up(0, k)
    for k in range(CHUNKS):
        act(0, k)
    loads[3].wait()
    for k in range(CHUNKS):
        down(0, k)
    for k in range(CHUNKS):
        scatter(0, k)
    for k in range(CHUNKS):
        spread(k)

    for k in range(CHUNKS):
        collect(k)
        prepare(1, k)
        up(1, k)
    for k in range(CHUNKS):
        act(1, k)
    for k in range(CHUNKS):
        down(1, k)
    for k in range(CHUNKS):
        scatter(1, k)

    chosen = jnp.zeros((8, 128), F32)
    for k in range(CHUNKS):
        state = new_state(1, k)
        t = lax.broadcasted_iota(jnp.int32, (8, 32), 1)
        beam_of = (8 * k + t // 4) * 8 + 4 * core + lax.rem(t, 4)
        picker = (kept[...] == beam_of).astype(F32).astype(BF)
        chosen = chosen + jnp.dot(picker, state.astype(BF), preferred_element_type=F32)
        dec_send[k] = state.reshape(4, 8, 128).astype(BF)
    pick[...] = chosen
    remote(pick, pick_sib, snd.at[7], pick_sib_sem.at[0], sibling).start()
    remote(pick, pick_sib, snd.at[7], pick_sib_sem.at[0], sibling).wait_recv()
    pick_all[chip] = chosen + pick_sib[...]
    piece = pick_all.at[chip]
    for d in CHIP_STEPS:
        remote(piece, piece, snd.at[8], pick_sem.at[d], to_chip(chip_at(d))).start()
    sent.append((pick, snd.at[7]))
    sent.append((pick_all.at[pl.ds(0, NQ - 1)], snd.at[8]))

    def rel(src, dst):
        return lax.rem(src - dst + NQ, NQ)

    for k in range(CHUNKS):
        for g in range(4):
            for b in range(2):
                q = 8 * k + 2 * g + b

                @pl.when(q != chip)
                def _():
                    remote(dec_send.at[k, g], dec_in.at[rel(chip, q)], snd.at[9], dec_sem.at[0], to_chip(q)).start()

                @pl.when(q == chip)
                def _():
                    dec_in[0] = dec_send[k, g]

    sent.append((dec_in.at[pl.ds(1, NQ - 1)], snd.at[9]))
    for d in reversed(CHIP_STEPS):
        arrived = pick_all.at[chip_from(d)]
        remote(arrived, arrived, snd.at[8], pick_sem.at[d], sibling).wait_recv()

    for k in range(CHUNKS):
        for h in range(2):
            for cb in range(NQ):
                cols = slice(cb * 128, cb * 128 + 128)
                w = words[h * 64 + 32 * k : h * 64 + 32 * k + 32, cols].astype(F32)
                c = jnp.concatenate(
                    [jnp.broadcast_to(pick_all[cb, 4 * k + g : 4 * k + g + 1], (8, 128)) for g in range(4)], axis=0
                )
                rows = (c + w).astype(BF)
                x[2, k, h, cb] = rows
                rows_f[h, 4 * k : 4 * k + 4, :, cols] = rows.astype(F32).reshape(4, 8, 128)
        prepare(2, k)
        up(2, k)

    arrived = dec_in.at[pl.ds(1, NQ - 1)]
    remote(arrived, arrived, snd.at[9], dec_sem.at[0], sibling).wait_recv()
    for cb in range(NQ):
        both = dec_in[rel(cb, chip)].astype(F32)
        dec_out[:, cb * 128 : cb * 128 + 128] = jnp.where(yh == 0, both[0:4], both[4:8]).astype(BF)

    for k in range(CHUNKS):
        act(2, k)
    for k in range(CHUNKS):
        down(2, k)
    for k in range(CHUNKS):
        i = 2 * CHUNKS + k
        remote(sib_in.at[2, k], sib_in.at[2, k], snd.at[30 + i], sib_sem.at[i], sibling).wait_recv()
        for n in range(8):
            left = own[k, n] + sib_in[2, k, n].astype(F32)
            right = own[k, n + 8] + sib_in[2, k, n + 8].astype(F32)
            for g in range(4):
                even, odd = halves(left[8 * g : 8 * g + 8], right[8 * g : 8 * g + 8])
                last[8 * k + 2 * g, :, n * 128 : n * 128 + 128] = even.astype(BF)
                last[8 * k + 2 * g + 1, :, n * 128 : n * 128 + 128] = odd.astype(BF)
        for g in range(4):
            for b in range(2):
                q = 8 * k + 2 * g + b

                @pl.when(q != chip)
                def _():
                    remote(last.at[q], last_in.at[rel(chip, q)], snd.at[40 + i], last_sem.at[0], to_chip(q)).start()

    @pl.when(chip < 8)
    def _():
        remote(last.at[pl.ds(0, 7)], last.at[pl.ds(0, 7)], snd.at[44], last_sem.at[0], sibling).wait_send()
        remote(last.at[pl.ds(8, 8)], last.at[pl.ds(8, 8)], snd.at[45], last_sem.at[0], sibling).wait_send()

    @pl.when(chip >= 8)
    def _():
        remote(last.at[pl.ds(0, 8)], last.at[pl.ds(0, 8)], snd.at[44], last_sem.at[0], sibling).wait_send()
        remote(last.at[pl.ds(8, 7)], last.at[pl.ds(8, 7)], snd.at[45], last_sem.at[0], sibling).wait_send()

    for ref, sem in sent:
        remote(ref, ref, sem, sem, sibling).wait_send()

    arrived = last_in.at[pl.ds(1, NQ - 1)]
    remote(arrived, arrived, snd.at[44], last_sem.at[0], sibling).wait_recv()
    total = last[chip].astype(F32)
    for s in range(1, NQ):
        total = total + last_in[s].astype(F32)
    mine = rows_f[core, z]
    even, odd = halves(mine[:, 0:1024], mine[:, 1024:2048])
    result = (jnp.where(yh == 0, even, odd) + total).astype(BF).astype(F32)
    ev_out[:, 0:1024] = result[0:4].astype(BF)
    ev_out[:, 1024:2048] = result[4:8].astype(BF)


def on_device(
    beam_states, step_tokens, norm_gain, w_gate, w_up, w_down, prompt_table, kept_beams, prompt_ids
):
    ids = prompt_ids.reshape(16, 2, 4).transpose(1, 0, 2).reshape(128, 1)
    vmem = pl.BlockSpec(memory_space=pltpu.VMEM)
    hbm = pl.BlockSpec(memory_space=pl.ANY)
    V, dma = pltpu.VMEM, pltpu.SemaphoreType.DMA
    n = LAYERS * CHUNKS
    scratch = [
        V((WIDTH, HID), BF), V((WIDTH, HID), BF), V((HID, WIDTH), BF), V((256, WIDTH), BF),
        V((128, WIDTH), BF),
        V((2, NQ, 8, 1024), BF),
        V((LAYERS, CHUNKS, 2, NQ, 32, 128), BF),
        V((64, WIDTH), BF),
        V((LAYERS, CHUNKS, 8, 16, 1024), BF), V((LAYERS, CHUNKS, 8, 16, 1024), BF),
        V((LAYERS, CHUNKS, 8, 8, HID), BF), V((64, HID), BF),
        V((CHUNKS, NQ, 32, 128), F32),
        V((LAYERS, CHUNKS, NQ, 32, 128), BF), V((LAYERS, CHUNKS, NQ, 32, 128), BF),
        V((2, CHUNKS, NQ, 32, 128), BF), V((2, CHUNKS, NQ, 32, 128), BF),
        V((NQ, 8, 128), BF), V((NQ, 8, 128), BF),
        V((8, 128), F32), V((8, 128), F32), V((NQ, 8, 128), F32),
        V((2, 8, 8, WIDTH), F32),
        V((CHUNKS, 4, 8, 128), BF), V((NQ, 8, 128), BF),
        V((NQ, 8, 1024), BF), V((NQ, 8, 1024), BF),
        dma((4,)), dma((50,)), dma((NQ,)), dma((1,)), dma((NQ,)),
        dma((CHUNKS, NQ)), dma((CHUNKS,)), dma((n,)), dma((n, 8)),
        dma((n,)), dma((n,)), dma((NQ,)), dma((1,)), dma((1,)), dma((1,)),
    ]
    return pl.pallas_call(
        kernel,
        out_shape=(jax.ShapeDtypeStruct((4, WIDTH), BF), jax.ShapeDtypeStruct((4, WIDTH), BF)),
        in_specs=[vmem] * 5 + [hbm] * 4,
        out_specs=(vmem, vmem),
        scratch_shapes=scratch,
        compiler_params=pltpu.CompilerParams(
            collective_id=0, has_side_effects=True, vmem_limit_bytes=48 * 2**20
        ),
        name="beam_steps",
    )(
        beam_states, step_tokens, norm_gain.reshape(1, WIDTH), kept_beams.reshape(8, 1), ids,
        w_gate, w_up, w_down, prompt_table,
    )


def solution(mesh):
    return jax.shard_map(
        on_device,
        mesh=mesh,
        in_specs=(
            P("gy", "gx"),
            P(None, "gy", "gx"),
            P("gx"),
            P("gx", "gy"),
            P("gx", "gy"),
            P("gy", "gx"),
            P(None, "gx"),
            P(),
            P(),
        ),
        out_specs=(P("gy", "gx"), P("gy", "gx")),
        check_vma=False,
    )
```

time: 239 us -> 118 us (0.49)
  blocking collectives: 133 us -> 0 us
  Pallas kernels: 0 us -> 108 us
  waiting for transfers between devices: 50.2 us -> 0 us
  starting transfers between devices: 27 us -> 0 us
  matrix products: 15.8 us -> 0 us
  other arithmetic: 4.57 us -> 0 us
    all_to_all x9 -> x0, blocking collectives: 133 us -> none  [the longest x5 85.3 us: sent_and_summed(): lax.all_to_all(cut_along(array, dim, peers), axis, 0, 0, tiled=True)]
    pallas_call x0 -> x1, Pallas kernels: none -> 108 us  [on_device(): pl.pallas_call(kernel, out_shape=(jax.ShapeDtypeStruct((4, WIDTH), BF), j...]
    all_to_all x3 -> x0, waiting for transfers between devices: 50.2 us -> none  [the longest x2 33.2 us: from_everyone(): return lax.all_to_all(copies, axis, split_axis=0, concat_axis=0, tiled=True)]
    all_to_all x3 -> x0, starting transfers between devices: 27 us -> none  [the longest x2 18.4 us: from_everyone(): return lax.all_to_all(copies, axis, split_axis=0, concat_axis=0, tiled=True)]
    dot_general x11 -> x0, matrix products: 15.8 us -> none  [the longest x3 6.56 us: layer_rows(): upper_part = jnp.dot(scaled, w_up, preferred_element_type=jnp.float32)]
    unnamed x20 -> x10, local copies, waits for them, and re-layouts: 2.17 us -> 5.96 us
    convert_element_type x8 -> x0, other arithmetic: 2.49 us -> none  [the longest x2 0.85 us: on_device(): (state.astype(jnp.float32) + step_tokens[step].astype(jnp.float32)).astyp...]
    broadcast_in_dim x7 -> x0, local copies, waits for them, and re-layouts: 2.44 us -> none  [the longest x6 2.34 us: from_everyone(): copies = jnp.broadcast_to(array, (lax.axis_size(axis), *array.shape))]
  transfers between devices with their start and end apart: 3 -> 0, of which waited for: 3 -> 0; matrix products, arithmetic and copies ran while one was open for 0% -> 0% of each run, Pallas kernels for 0% -> 0%
where the time goes in v1:
time: 118 us; the launch traced here: 117 us
  Pallas kernels  108 us (92%)
  local copies, waits for them, and re-layouts  8.22 us (7%)
    pallas_call x1, Pallas kernels, on_device(): pl.pallas_call(kernel, out_shape=(jax.ShapeDtypeStruct((4, WIDTH), BF), j...  108 us
    unnamed x10, local copies, waits for them, and re-layouts  5.96 us

profile of v1, /device:TPU:1, one launch (start us, length us, event | category | flops | bytes accessed | tf_op | source)
XLA Modules:
  0.0 117.3 jit_solution(159420091863047549)
XLA Ops:
  0.6 0.7 copy.15.kept
  1.4 0.7 reshape.16.gain
  2.1 0.8 reshape.18
  2.8 0.1 reshape.20.ids
  2.9 0.0 copy-start
  2.9 2.0 %copy-done = bf16[2048,896]{1,0:T(8,128)(2,1)S(1)} copy-done((bf16[2048,896]{1,0:T(8,128)(2,1)S(1)}, bf16[2048,896]{1,0:T(8,128)(2,1)}, u32[]{:S(2)}) %copy-start) | copy-done | bytes 3670040
  5.0 0.0 copy-start.1
  5.0 1.2 %copy-done.1 = bf16[256,2048]{1,0:T(8,128)(2,1)S(1)} copy-done((bf16[256,2048]{1,0:T(8,128)(2,1)S(1)}, bf16[256,2048]{1,0:T(8,128)(2,1)}, u32[]{:S(2)}) %copy-start.1) | copy-done | bytes 1048600
  6.2 0.0 copy-start.2
  6.2 0.8 copy-done.2
  6.9 0.0 copy-start.3
  6.9 0.7 copy-done.3
  7.7 108.4 %beam_steps.1 = (bf16[4,2048]{1,0:T(4,128)(2,1)S(1)}, bf16[4,2048]{1,0:T(4,128)(2,1)S(1)}) custom-call(bf16[4,2048]{1,0:T(4,128)(2,1)S(1)} %copy-done.3, bf16[2,4,2048]{2,1,0:T(4,128)(2,1)S(1)} %copy-done.2, bf16[1,2048]{1,0:T(2,128)(2,1)S(1)} %reshape.16.gain, s32[8,1]{1,0:T(8,128)S(1)} %copy.15.kept, s32[128,1]{1,0:T(8,128)S(1)} %reshape.20.ids, ...), custom_call_target="tpu_custom_call" | custom-call | tf_op jit(solution)/shard_map/beam_steps/pallas_call | solution.py:404
  116.1 0.6 copy.19
  116.7 0.6 copy.20
  (1 shorter events, 0.0 us)
Async XLA Ops:
  2.9 2.0 %copy-start = (bf16[2048,896]{1,0:T(8,128)(2,1)S(1)}, bf16[2048,896]{1,0:T(8,128)(2,1)}, u32[]{:S(2)}) copy-start(bf16[2048,896]{1,0:T(8,128)(2,1)} %wg_hbm.1) | copy-start | bytes 11010052
  5.0 1.2 %copy-start.1 = (bf16[256,2048]{1,0:T(8,128)(2,1)S(1)}, bf16[256,2048]{1,0:T(8,128)(2,1)}, u32[]{:S(2)}) copy-start(bf16[256,2048]{1,0:T(8,128)(2,1)} %tab_hbm.1) | copy-start | bytes 3145732
  6.2 0.8 copy-start.2
  6.9 0.7 copy-start.3

commit v2 on v1

v2 whole, which is shorter than its diff:
```python
import jax
import jax.numpy as jnp
from jax import lax
from jax.experimental import pallas as pl
from jax.experimental.pallas import tpu as pltpu
from jax.sharding import PartitionSpec as P

D = 16384
EPS = 1e-05
BF, F32 = jnp.bfloat16, jnp.float32
NX, NY = 4, 2
NQ = 16
WIDTH = 2048
HID = 896
LAYERS, CHUNKS = 3, 2
MESH = pl.DeviceIdType.MESH

CHIP_STEPS = sorted(range(1, NQ), key=lambda d: -(min(d // 2, 8 - d // 2) + 2 * (d % 2)))
GX_STEPS = sorted(range(1, 8), key=lambda e: -(min(e % 4, 4 - e % 4) + e // 4))


def swap(a, b, rows):
    first = lax.rem(lax.broadcasted_iota(jnp.int32, a.shape, 0), 2 * rows) < rows
    return jnp.where(first, a, pltpu.roll(b, rows, 0)), jnp.where(first, pltpu.roll(a, 8 - rows, 0), b)


def turn(a):
    a0, a2 = swap(a[0], a[2], 4)
    a1, a3 = swap(a[1], a[3], 4)
    return (*swap(a0, a1, 2), *swap(a2, a3, 2))


def kernel(
    beam_hbm, tok_hbm, gain_hbm, kept_hbm, ids_hbm, wg_hbm, wu_hbm, wd_hbm, tab_hbm,
    dec_out, ev_out,
    beam, tok, gain, kept, ids, wg, wu, wd, tab, words, first, x, xs, part, part_in, hid, hid_mm,
    own, sib_out, sib_in, sums, sums_in, tok_out, tok_in,
    kp, kp_out, kp_in, ks, ks_in, pick_all, rows_f, dec_send, dec_in, last, last_in,
    load_sem, snd, first_sem, first_fwd, tok_sem, ag_sem, ag_fwd, rsx_sem, agx_sem,
    sib_sem, rsy_sem, kp_sem, ks_sem, pick_sem, dec_sem, last_sem,
):
    gx, gy = lax.axis_index("gx"), lax.axis_index("gy")
    px, pyl = lax.rem(gx, NX), gx // NX
    core, chip = lax.rem(gy, 2), gy // 2
    yh, z = lax.rem(chip, 2), chip // 2
    other = 1 - core
    sibling = (gx, chip * 2 + other)

    def chip_at(d):
        return lax.rem(z + d // 2, 8) * 2 + lax.rem(yh + d % 2, 2)

    def chip_from(d):
        return lax.rem(z + 8 - d // 2, 8) * 2 + lax.rem(yh + d % 2, 2)

    def gx_at(e):
        return lax.rem(pyl + e // 4, NY) * NX + lax.rem(px + e % 4, NX)

    def gx_from(e):
        return lax.rem(pyl + e // 4, NY) * NX + lax.rem(px + 4 - e % 4, NX)

    def to_chip(q):
        return (gx, q * 2 + core)

    def to_gx(p):
        return (p, gy)

    def remote(src, dst, send, recv, device):
        return pltpu.make_async_remote_copy(
            src_ref=src, dst_ref=dst, send_sem=send, recv_sem=recv, device_id=device, device_id_type=MESH
        )

    def arrived(ref, recv):
        remote(ref, ref, snd.at[0], recv, sibling).wait_recv()

    sent = []

    def sending(ref):
        sent.append(ref)
        return snd.at[len(sent) - 1]

    pairs = [
        (beam_hbm, beam), (tok_hbm, tok), (tab_hbm, tab), (ids_hbm, ids), (kept_hbm, kept), (gain_hbm, gain),
        (wg_hbm, wg), (wu_hbm, wu), (wd_hbm, wd),
    ]
    loads = [pltpu.make_async_copy(s, d, load_sem.at[i]) for i, (s, d) in enumerate(pairs)]
    for load in loads:
        load.start()

    barrier = pltpu.get_barrier_semaphore()
    for d in CHIP_STEPS:
        pl.semaphore_signal(barrier, inc=1, device_id=to_chip(chip_at(d)), device_id_type=MESH)
    for e in GX_STEPS:
        pl.semaphore_signal(barrier, inc=1, device_id=to_gx(gx_at(e)), device_id_type=MESH)
    pl.semaphore_signal(barrier, inc=1, device_id=sibling, device_id_type=MESH)

    loads[0].wait()
    loads[1].wait()
    mixed = (beam[...].astype(F32) + tok[0].astype(F32)).astype(BF).astype(F32)
    mixed = jnp.concatenate([mixed, mixed], axis=0)
    top = lax.broadcasted_iota(jnp.int32, (8, 512), 0) < 4
    even, odd = swap(
        jnp.where(top, mixed[:, 0:512], mixed[:, 1024:1536]), jnp.where(top, mixed[:, 512:1024], mixed[:, 1536:2048]), 2
    )
    first[0, core, chip] = even.astype(BF)
    first[1, core, chip] = odd.astype(BF)
    token = tok[1].astype(F32)
    token = jnp.concatenate([token, token], axis=0).astype(BF)
    for cb in range(NQ):
        tok_out[cb] = token[:, cb * 128 : cb * 128 + 128]

    pl.semaphore_wait(barrier, NQ - 1 + 7 + 1)

    forward = []
    for k in range(CHUNKS):
        piece = first.at[k, core, chip]
        sem = sending(first.at[k, 0, pl.ds(0, NQ - 1)])
        forward.append(sending(first.at[k, 0]))
        for d in CHIP_STEPS:
            remote(piece, piece, sem, first_sem.at[k, d], to_chip(chip_at(d))).start()
        remote(piece, piece, forward[k], first_fwd.at[k], sibling).start()
    sem = sending(tok_in.at[pl.ds(0, NQ - 1)])
    for d in CHIP_STEPS:
        remote(tok_out.at[chip_at(d)], tok_in.at[chip], sem, tok_sem.at[d], to_chip(chip_at(d))).start()
    tok_in[chip] = tok_out[chip]

    for load in loads[2:6]:
        load.wait()

    def row_of(shape, dim):
        t = lax.broadcasted_iota(jnp.int32, shape, dim)
        return 8 * (lax.rem(t, 32) // 2) + 4 * (lax.rem(t, 64) // 32) + 2 * (t // 64) + lax.rem(t, 2)

    of_beam = (row_of((128, 8), 0) // 16 == lax.broadcasted_iota(jnp.int32, (128, 8), 1)).astype(F32).astype(BF)
    beam_ids = jnp.dot(of_beam, ids[...].astype(F32).astype(BF), preferred_element_type=F32)
    place = lax.rem(row_of((128, 16), 0), 16) == lax.broadcasted_iota(jnp.int32, (128, 16), 1)
    row_ids = jnp.sum(jnp.where(place, beam_ids, 0.0), axis=1, keepdims=True)
    lookup = (row_ids == lax.broadcasted_iota(jnp.int32, (128, 256), 1).astype(F32)).astype(F32).astype(BF)
    for n in range(4):
        cols = slice(n * 512, n * 512 + 512)
        words[:, cols] = jnp.dot(lookup, tab[:, cols], preferred_element_type=F32).astype(BF)
    nth = lax.broadcasted_iota(jnp.int32, (16, 128), 0)
    kept_rows = jnp.full((16, 128), -1, jnp.int32)
    for n in range(8):
        kept_rows = jnp.where(nth == n, kept[n], kept_rows)
    picker = (kept_rows == row_of((16, 128), 1)).astype(F32).astype(BF)

    def prepare(layer, k):
        squares = []
        for h in range(2):
            total = jnp.zeros((32, 128), F32)
            for cb in range(NQ):
                v = x[layer, k, h, cb].astype(F32)
                total = total + v * v
                cols = slice(cb * 128, cb * 128 + 128)
                xs[h * 32 : h * 32 + 32, cols] = (v * gain[cols].astype(F32)[None, :]).astype(BF)
            squares.append(jnp.sum(total, axis=1, keepdims=True))
        whole = jnp.broadcast_to(jnp.concatenate(squares, axis=0), (64, 128))
        high = whole.astype(BF).astype(F32)
        both = jnp.concatenate([high.reshape(8, 8, 128), (whole - high).reshape(8, 8, 128)], axis=1)
        part[layer, k, :, :, HID:1024] = both.astype(BF)

    def up(layer, k):
        rows = xs[...]

        def tile(n, carry):
            cols = pl.ds(pl.multiple_of(n * 128, 128), 128)
            weights = jnp.concatenate([wg[:, cols], wu[:, cols]], axis=1)
            y = jnp.dot(rows, weights, preferred_element_type=F32)
            both = jnp.concatenate([y[:, :128].reshape(8, 8, 128), y[:, 128:].reshape(8, 8, 128)], axis=1)
            part[layer, k, :, :, cols] = both.astype(BF)
            return carry

        lax.fori_loop(0, HID // 128, tile, 0)
        sem = sending(part_in.at[layer, k, pl.ds(1, 7)])
        for e in GX_STEPS:
            p = gx_at(e)
            remote(part.at[layer, k, p], part_in.at[layer, k, e], sem, rsx_sem.at[layer, k], to_gx(p)).start()

    def act(layer, k):
        arrived(part_in.at[layer, k, pl.ds(1, 7)], rsx_sem.at[layer, k])
        total = part[layer, k, gx].astype(F32)
        for e in range(1, 8):
            total = total + part_in[layer, k, e].astype(F32)
        squares = total[0:8, HID:1024] + total[8:16, HID:1024]
        scale = lax.rsqrt(squares / D + EPS)
        for n in range(HID // 128):
            cols = slice(n * 128, n * 128 + 128)
            g = scale * total[0:8, cols]
            u = scale * total[8:16, cols]
            hid[layer, k, gx, :, cols] = (g / (1.0 + jnp.exp(-g)) * u).astype(BF)
        piece = hid.at[layer, k, gx]
        sem = sending(hid.at[layer, k, pl.ds(0, 7)])
        for e in GX_STEPS:
            remote(piece, piece, sem, agx_sem.at[layer, k, e], to_gx(gx_at(e))).start()

    def hidden(layer, k):
        for e in reversed(GX_STEPS):
            arrived(hid.at[layer, k, gx_from(e)], agx_sem.at[layer, k, e])
        hid_mm[k, 0:64] = hid[layer, k].astype(F32).reshape(64, HID).astype(BF)

    def down(layer, k, with_kept=False):
        rows = hid_mm[k] if with_kept else hid_mm[k, 0:64]

        def tile(n, carry):
            cols = pl.ds(pl.multiple_of(n * 256, 128), 256)
            y = jnp.dot(rows, wd[:, cols], preferred_element_type=F32)
            mine = jnp.where(core == 0, y[0:32], y[32:64])
            theirs = jnp.where(core == 0, y[32:64], y[0:32]).astype(BF)
            for m in range(2):
                own[layer, k, 2 * n + m] = mine[:, m * 128 : m * 128 + 128]
                sib_out[layer, k, 2 * n + m] = theirs[:, m * 128 : m * 128 + 128]
                if with_kept:
                    kp[2 * n + m] = y[64:72, m * 128 : m * 128 + 128]
            return carry

        lax.fori_loop(0, 8, tile, 0)
        if with_kept:
            kp_out[...] = kp[pl.ds(8 * other, 8)].astype(BF)
            remote(kp_out, kp_in, sending(kp_out), kp_sem.at[0], sibling).start()
        sem = sending(sib_out.at[layer, k])
        remote(sib_out.at[layer, k], sib_in.at[layer, k], sem, sib_sem.at[layer, k], sibling).start()

    def scatter(layer, k):
        arrived(sib_in.at[layer, k], sib_sem.at[layer, k])
        sem = sending(sums_in.at[layer, k, pl.ds(1, NQ - 1)])
        for d in CHIP_STEPS:
            q = chip_at(d)
            sums[layer, k, q] = (own[layer, k, q] + sib_in[layer, k, q].astype(F32)).astype(BF)
            remote(sums.at[layer, k, q], sums_in.at[layer, k, d], sem, rsy_sem.at[layer, k], to_chip(q)).start()

    def new_state(layer, k):
        arrived(sums_in.at[layer, k, pl.ds(1, NQ - 1)], rsy_sem.at[layer, k])
        total = own[layer, k, chip] + sib_in[layer, k, chip].astype(F32)
        for d in range(1, NQ):
            total = total + sums_in[layer, k, d].astype(F32)
        return (x[layer, k, core, chip].astype(F32) + total).astype(BF).astype(F32)

    second_fwd = []

    def spread(k):
        state = new_state(0, k)
        if k == 0:
            for d in CHIP_STEPS:
                arrived(tok_in.at[chip_from(d)], tok_sem.at[d])
        pair = lax.broadcasted_iota(jnp.int32, (8, 128), 0) // 2
        groups = []
        for g in range(4):
            group = jnp.zeros((8, 128), F32)
            for a in range(4):
                t = tok_in[4 * g + a].astype(F32)
                group = jnp.where(pair == a, t if a % 2 == k else pltpu.roll(t, 2, 0), group)
            groups.append(group)
        x[1, k, core, chip] = (state + jnp.concatenate(groups, axis=0)).astype(BF)
        piece = x.at[1, k, core, chip]
        sem = sending(x.at[1, k, 0, pl.ds(0, NQ - 1)])
        second_fwd.append(sending(x.at[1, k, 0]))
        for d in CHIP_STEPS:
            remote(piece, piece, sem, ag_sem.at[k, d], to_chip(chip_at(d))).start()
        remote(piece, piece, second_fwd[k], ag_fwd.at[k], sibling).start()

    def collect(k):
        for d in reversed(CHIP_STEPS):
            piece = x.at[1, k, core, chip_from(d)]
            arrived(piece, ag_sem.at[k, d])
            remote(piece, piece, second_fwd[k], ag_fwd.at[k], sibling).start()
        arrived(x.at[1, k, other], ag_fwd.at[k])

    for k in range(CHUNKS):
        for d in reversed(CHIP_STEPS):
            piece = first.at[k, core, chip_from(d)]
            arrived(piece, first_sem.at[k, d])
            remote(piece, piece, forward[k], first_fwd.at[k], sibling).start()
        arrived(first.at[k, other], first_fwd.at[k])
        for h in range(2):
            for g in range(4):
                quarters = turn([first[k, h, 4 * g + a].astype(F32) for a in range(4)])
                for m in range(4):
                    rows_f[k, h, g, :, m * 512 : m * 512 + 512] = quarters[m]
            for cb in range(NQ):
                block = rows_f[k, h, :, :, cb * 128 : cb * 128 + 128]
                x[0, k, h, cb] = block.reshape(32, 128).astype(BF)
        prepare(0, k)
        if k == 0:
            loads[6].wait()
            loads[7].wait()
        up(0, k)
    for k in range(CHUNKS):
        act(0, k)
    loads[8].wait()
    for k in range(CHUNKS):
        hidden(0, k)
        down(0, k)
    for k in range(CHUNKS):
        scatter(0, k)
    for k in range(CHUNKS):
        spread(k)

    for k in range(CHUNKS):
        collect(k)
        prepare(1, k)
        up(1, k)
    for k in range(CHUNKS):
        act(1, k)
    kept_mixed = []
    for m in range(8):
        cb = 8 * core + m
        column = jnp.concatenate([x[1, k, h, cb] for k in range(CHUNKS) for h in range(2)], axis=0)
        kept_mixed.append(jnp.dot(picker, column, preferred_element_type=F32)[0:8])
    for k in range(CHUNKS):
        hidden(1, k)

    def pick_hidden(n, carry):
        cols = pl.ds(pl.multiple_of(n * 128, 128), 128)
        chosen = jnp.zeros((16, 128), F32)
        for k in range(CHUNKS):
            rows = picker[:, 64 * k : 64 * k + 64]
            chosen = chosen + jnp.dot(rows, hid_mm[k, 0:64, cols], preferred_element_type=F32)
        hid_mm[1, 64:80, cols] = chosen.astype(BF)
        return carry

    lax.fori_loop(0, HID // 128, pick_hidden, 0)
    down(1, 1, True)
    down(1, 0)

    arrived(kp_in, kp_sem.at[0])
    ks[...] = (kp[pl.ds(8 * core, 8)] + kp_in[...].astype(F32)).astype(BF)
    sem = sending(ks_in.at[pl.ds(1, NQ - 1)])
    for d in CHIP_STEPS:
        remote(ks, ks_in.at[d], sem, ks_sem.at[0], to_chip(chip_at(d))).start()
    arrived(ks_in.at[pl.ds(1, NQ - 1)], ks_sem.at[0])
    total = ks[...].astype(F32)
    for d in range(1, NQ):
        total = total + ks_in[d].astype(F32)
    for m in range(8):
        pick_all[8 * core + m] = (kept_mixed[m] + total[m]).astype(BF)
    half = pick_all.at[pl.ds(8 * core, 8)]
    remote(half, half, sending(half), pick_sem.at[0], sibling).start()
    arrived(half, pick_sem.at[0])

    upper = lax.broadcasted_iota(jnp.int32, (8, 128), 0) < 4
    for k in range(CHUNKS):
        for cb in range(NQ):
            cols = slice(cb * 128, cb * 128 + 128)
            chosen = pick_all[cb].astype(F32)
            chosen = jnp.concatenate(
                [jnp.where(upper, chosen[2 * g : 2 * g + 1], chosen[2 * g + 1 : 2 * g + 2]) for g in range(4)], axis=0
            )
            for h in range(2):
                at = 64 * k + 32 * h
                rows = (chosen + words[at : at + 32, cols].astype(F32)).astype(BF)
                x[2, k, h, cb] = rows
                rows_f[k, h, :, :, cols] = rows.astype(F32).reshape(4, 8, 128)
        prepare(2, k)
        up(2, k)

    for k in range(CHUNKS):
        scatter(1, k)
    for k in range(CHUNKS):
        act(2, k)
    for k in range(CHUNKS):
        state = new_state(1, k).reshape(4, 8, 128)
        dec_send[:, 8 * k : 8 * k + 8, :] = state.astype(BF)
    sem = sending(dec_in.at[pl.ds(1, NQ - 1)])
    for d in CHIP_STEPS:
        q = chip_at(d)
        remote(dec_send.at[q // 4], dec_in.at[d], sem, dec_sem.at[0], to_chip(q)).start()
    dec_in[0] = dec_send[chip // 4]

    for k in range(CHUNKS):
        hidden(2, k)
        down(2, k)
    for k in range(CHUNKS):
        arrived(sib_in.at[2, k], sib_sem.at[2, k])
        for n in range(4):
            blocks = [own[2, k, 4 * m + n] + sib_in[2, k, 4 * m + n].astype(F32) for m in range(4)]
            for g in range(4):
                turned = turn([b[8 * g : 8 * g + 8] for b in blocks])
                for a in range(4):
                    last[k, 4 * g + a, :, n * 128 : n * 128 + 128] = turned[a].astype(BF)
        sem = sending(last_in.at[k, pl.ds(1, NQ - 1)])
        for d in CHIP_STEPS:
            q = chip_at(d)
            remote(last.at[k, q], last_in.at[k, d], sem, last_sem.at[k], to_chip(q)).start()

    arrived(dec_in.at[pl.ds(1, NQ - 1)], dec_sem.at[0])
    quarter = lax.rem(chip, 4)

    def own_pair(block):
        block = jnp.where(quarter >= 2, pltpu.roll(block, 4, 0), block)
        return jnp.where(lax.rem(quarter, 2) == 1, pltpu.roll(block, 6, 0), block)

    for cb in range(NQ):
        step = lax.rem(z + 8 - cb // 2, 8) * 2 + lax.rem(yh + cb % 2, 2)
        both = dec_in[step].astype(F32)
        low, high = own_pair(both[0:8]), pltpu.roll(own_pair(both[8:16]), 2, 0)
        rows = jnp.where(lax.broadcasted_iota(jnp.int32, (8, 128), 0) < 2, low, high)
        dec_out[:, cb * 128 : cb * 128 + 128] = rows[0:4].astype(BF)

    results = []
    for k in range(CHUNKS):
        mine = rows_f[k, core, chip // 4]
        turned = turn([mine[:, m * 512 : m * 512 + 512] for m in range(4)])
        total = jnp.where(quarter == 0, turned[0], turned[1])
        total = jnp.where(quarter == 2, turned[2], total)
        total = jnp.where(quarter == 3, turned[3], total)
        results.append(total)
    for i, ref in enumerate(sent):
        remote(ref, ref, snd.at[i], snd.at[i], sibling).wait_send()
    for k in range(CHUNKS):
        arrived(last_in.at[k, pl.ds(1, NQ - 1)], last_sem.at[k])
        total = last[k, chip].astype(F32)
        for d in range(1, NQ):
            total = total + last_in[k, d].astype(F32)
        results[k] = (results[k] + total).astype(BF).astype(F32)
    even, odd = swap(results[0], results[1], 2)
    ev_out[:, 0:512] = even[0:4].astype(BF)
    ev_out[:, 512:1024] = odd[0:4].astype(BF)
    ev_out[:, 1024:1536] = even[4:8].astype(BF)
    ev_out[:, 1536:2048] = odd[4:8].astype(BF)


def on_device(
    beam_states, step_tokens, norm_gain, w_gate, w_up, w_down, prompt_table, kept_beams, prompt_ids
):
    vmem = pl.BlockSpec(memory_space=pltpu.VMEM)
    hbm = pl.BlockSpec(memory_space=pltpu.HBM)
    V, dma = pltpu.VMEM, pltpu.SemaphoreType.DMA
    LK = (LAYERS, CHUNKS)
    scratch = [
        V((4, WIDTH), BF), V((2, 4, WIDTH), BF), V((WIDTH,), BF), pltpu.SMEM((8,), jnp.int32), V((8, 16), jnp.int32),
        V((WIDTH, HID), BF), V((WIDTH, HID), BF), V((HID, WIDTH), BF), V((256, WIDTH), BF),
        V((128, WIDTH), BF),
        V((CHUNKS, 2, NQ, 8, 512), BF),
        V((*LK, 2, NQ, 32, 128), BF),
        V((64, WIDTH), BF),
        V((*LK, 8, 16, 1024), BF), V((*LK, 8, 16, 1024), BF),
        V((*LK, 8, 8, HID), BF), V((CHUNKS, 80, HID), BF),
        V((*LK, NQ, 32, 128), F32),
        V((*LK, NQ, 32, 128), BF), V((*LK, NQ, 32, 128), BF),
        V((2, CHUNKS, NQ, 32, 128), BF), V((2, CHUNKS, NQ, 32, 128), BF),
        V((NQ, 8, 128), BF), V((NQ, 8, 128), BF),
        V((NQ, 8, 128), F32), V((8, 8, 128), BF), V((8, 8, 128), BF),
        V((8, 8, 128), BF), V((NQ, 8, 8, 128), BF), V((NQ, 8, 128), BF),
        V((CHUNKS, 2, 4, 8, WIDTH), F32),
        V((4, 16, 128), BF), V((NQ, 16, 128), BF),
        V((CHUNKS, NQ, 8, 512), BF), V((CHUNKS, NQ, 8, 512), BF),
        dma((9,)), dma((48,)), dma((CHUNKS, NQ)), dma((CHUNKS,)), dma((NQ,)),
        dma((CHUNKS, NQ)), dma((CHUNKS,)), dma(LK), dma((*LK, 8)),
        dma(LK), dma(LK), dma((1,)), dma((1,)), dma((1,)), dma((1,)), dma((CHUNKS,)),
    ]
    return pl.pallas_call(
        kernel,
        out_shape=(jax.ShapeDtypeStruct((4, WIDTH), BF), jax.ShapeDtypeStruct((4, WIDTH), BF)),
        in_specs=[hbm] * 9,
        out_specs=(vmem, vmem),
        scratch_shapes=scratch,
        compiler_params=pltpu.CompilerParams(
            collective_id=0, has_side_effects=True, vmem_limit_bytes=56 * 2**20
        ),
        name="beam_steps",
    )(
        beam_states, step_tokens, norm_gain, kept_beams, prompt_ids,
        w_gate, w_up, w_down, prompt_table,
    )


def solution(mesh):
    return jax.shard_map(
        on_device,
        mesh=mesh,
        in_specs=(
            P("gy", "gx"),
            P(None, "gy", "gx"),
            P("gx"),
            P("gx", "gy"),
            P("gx", "gy"),
            P("gy", "gx"),
            P(None, "gx"),
            P(),
            P(),
        ),
        out_specs=(P("gy", "gx"), P("gy", "gx")),
        check_vma=False,
    )
```

time: 118 us -> 113 us (0.958)
  local copies, waits for them, and re-layouts: 8.22 us -> 2.66 us
  Pallas kernels: 108 us -> 110 us
    unnamed x10 -> x2, local copies, waits for them, and re-layouts: 5.96 us -> 2.66 us
    reshape x4 -> x0, local copies, waits for them, and re-layouts: 2.26 us -> none  [the longest x2 0.84 us: on_device(): ids = prompt_ids.reshape(16, 2, 4).transpose(1, 0, 2).reshape(128, 1)]
where the time goes in v2:
time: 113 us
  Pallas kernels  110 us (97%)
  local copies, waits for them, and re-layouts  2.66 us (2%)
    pallas_call x1, Pallas kernels, on_device(): pl.pallas_call(kernel, out_shape=(jax.ShapeDtypeStruct((4, WIDTH), BF), j...  110 us
    unnamed x2, local copies, waits for them, and re-layouts  2.66 us

profile of v2, /device:TPU:1, one launch (start us, length us, event | category | flops | bytes accessed | tf_op | source)
XLA Modules:
  0.0 112.9 jit_solution(1144544970716655588)
XLA Ops:
  0.6 109.6 %beam_steps.1 = (bf16[4,2048]{1,0:T(4,128)(2,1)}, bf16[4,2048]{1,0:T(4,128)(2,1)}) custom-call(bf16[4,2048]{1,0:T(4,128)(2,1)} %beam_hbm.1, bf16[2,4,2048]{2,1,0:T(4,128)(2,1)} %tok_hbm.1, bf16[2048]{0:T(1024)(128)(2,1)} %gain_hbm.1, s32[8]{0:T(128)} %kept_hbm.1, s32[8,16]{1,0:T(8,128)} %ids_hbm.1, bf16[2048,896]{1,0:T(8,128)(2,1)} %wg_hbm.1, ...), custom_call_target="tpu_custom_call" | custom-call | tf_op jit(solution)/shard_map/beam_steps/pallas_call | solution.py:451
  110.2 1.3 %copy.13 = bf16[4,2048]{1,0:T(4,128)(2,1)} copy(bf16[4,2048]{1,0:T(4,128)(2,1)} %get-tuple-element.4) | data formatting | bytes 32768
  111.5 1.3 %copy.14 = bf16[4,2048]{1,0:T(4,128)(2,1)} copy(bf16[4,2048]{1,0:T(4,128)(2,1)} %get-tuple-element.5) | data formatting | bytes 32768

commit v3 on v2

--- a/solution.py
+++ b/solution.py
@@ -160,17 +160,12 @@
         part[layer, k, :, :, HID:1024] = both.astype(BF)
 
     def up(layer, k):
-        rows = xs[...]
-
-        def tile(n, carry):
-            cols = pl.ds(pl.multiple_of(n * 128, 128), 128)
+        for n in range(HID // 128):
+            cols = slice(n * 128, n * 128 + 128)
             weights = jnp.concatenate([wg[:, cols], wu[:, cols]], axis=1)
-            y = jnp.dot(rows, weights, preferred_element_type=F32)
+            y = jnp.dot(xs[...], weights, preferred_element_type=F32)
             both = jnp.concatenate([y[:, :128].reshape(8, 8, 128), y[:, 128:].reshape(8, 8, 128)], axis=1)
             part[layer, k, :, :, cols] = both.astype(BF)
-            return carry
-
-        lax.fori_loop(0, HID // 128, tile, 0)
         sem = sending(part_in.at[layer, k, pl.ds(1, 7)])
         for e in GX_STEPS:
             p = gx_at(e)
@@ -199,11 +194,9 @@
         hid_mm[k, 0:64] = hid[layer, k].astype(F32).reshape(64, HID).astype(BF)
 
     def down(layer, k, with_kept=False):
-        rows = hid_mm[k] if with_kept else hid_mm[k, 0:64]
-
-        def tile(n, carry):
-            cols = pl.ds(pl.multiple_of(n * 256, 128), 256)
-            y = jnp.dot(rows, wd[:, cols], preferred_element_type=F32)
+        for n in range(8):
+            rows = hid_mm[k] if with_kept else hid_mm[k, 0:64]
+            y = jnp.dot(rows, wd[:, n * 256 : n * 256 + 256], preferred_element_type=F32)
             mine = jnp.where(core == 0, y[0:32], y[32:64])
             theirs = jnp.where(core == 0, y[32:64], y[0:32]).astype(BF)
             for m in range(2):
@@ -211,9 +204,6 @@
                 sib_out[layer, k, 2 * n + m] = theirs[:, m * 128 : m * 128 + 128]
                 if with_kept:
                     kp[2 * n + m] = y[64:72, m * 128 : m * 128 + 128]
-            return carry
-
-        lax.fori_loop(0, 8, tile, 0)
         if with_kept:
             kp_out[...] = kp[pl.ds(8 * other, 8)].astype(BF)
             remote(kp_out, kp_in, sending(kp_out), kp_sem.at[0], sibling).start()

time: 113 us -> 106 us (0.938)
  Pallas kernels: 110 us -> 102 us
    pallas_call x1, Pallas kernels: 110 us -> 102 us  [on_device(): pl.pallas_call(kernel, out_shape=(jax.ShapeDtypeStruct((4, WIDTH), BF), j...]
where the time goes in v3:
time: 106 us; the launch traced here: 105 us
  Pallas kernels  102 us (96%)
  local copies, waits for them, and re-layouts  2.66 us (3%)
    pallas_call x1, Pallas kernels, on_device(): pl.pallas_call(kernel, out_shape=(jax.ShapeDtypeStruct((4, WIDTH), BF), j...  102 us
    unnamed x2, local copies, waits for them, and re-layouts  2.66 us

profile of v3, /device:TPU:1, one launch (start us, length us, event | category | flops | bytes accessed | tf_op | source)
XLA Modules:
  0.0 105.3 jit_solution(17983732931550604407)
XLA Ops:
  0.6 102.0 %beam_steps.1 = (bf16[4,2048]{1,0:T(4,128)(2,1)}, bf16[4,2048]{1,0:T(4,128)(2,1)}) custom-call(bf16[4,2048]{1,0:T(4,128)(2,1)} %beam_hbm.1, bf16[2,4,2048]{2,1,0:T(4,128)(2,1)} %tok_hbm.1, bf16[2048]{0:T(1024)(128)(2,1)} %gain_hbm.1, s32[8]{0:T(128)} %kept_hbm.1, s32[8,16]{1,0:T(8,128)} %ids_hbm.1, bf16[2048,896]{1,0:T(8,128)(2,1)} %wg_hbm.1, ...), custom_call_target="tpu_custom_call" | custom-call | tf_op jit(solution)/shard_map/beam_steps/pallas_call | solution.py:441
  102.7 1.3 %copy.13 = bf16[4,2048]{1,0:T(4,128)(2,1)} copy(bf16[4,2048]{1,0:T(4,128)(2,1)} %get-tuple-element.4) | data formatting | bytes 32768
  104.0 1.3 %copy.14 = bf16[4,2048]{1,0:T(4,128)(2,1)} copy(bf16[4,2048]{1,0:T(4,128)(2,1)} %get-tuple-element.5) | data formatting | bytes 32768

commit v4 on v3

--- a/solution.py
+++ b/solution.py
@@ -16,6 +16,8 @@
 MESH = pl.DeviceIdType.MESH
 
 CHIP_STEPS = sorted(range(1, NQ), key=lambda d: -(min(d // 2, 8 - d // 2) + 2 * (d % 2)))
+Z_STEPS = (4, 3, 5, 2, 6, 1, 7, 0)
+BLOCK_PAIRS = (0, 2, 4, 6, 1, 3, 5, 7)
 GX_STEPS = sorted(range(1, 8), key=lambda e: -(min(e % 4, 4 - e % 4) + e // 4))
 
 
@@ -35,9 +37,9 @@
     dec_out, ev_out,
     beam, tok, gain, kept, ids, wg, wu, wd, tab, words, first, x, xs, part, part_in, hid, hid_mm,
     own, sib_out, sib_in, sums, sums_in, tok_out, tok_in,
-    kp, kp_out, kp_in, ks, ks_in, pick_all, rows_f, dec_send, dec_in, last, last_in,
+    kp, kp_out, kp_in, ks, ks_in, pick_all, rows_f, tokens, last, last_in,
     load_sem, snd, first_sem, first_fwd, tok_sem, ag_sem, ag_fwd, rsx_sem, agx_sem,
-    sib_sem, rsy_sem, kp_sem, ks_sem, pick_sem, dec_sem, last_sem,
+    sib_sem, rsy_sem, kp_sem, ks_sem, pick_sem, last_sem,
 ):
     gx, gy = lax.axis_index("gx"), lax.axis_index("gy")
     px, pyl = lax.rem(gx, NX), gx // NX
@@ -194,53 +196,110 @@
         hid_mm[k, 0:64] = hid[layer, k].astype(F32).reshape(64, HID).astype(BF)
 
     def down(layer, k, with_kept=False):
-        for n in range(8):
+        for j in range(8):
+            pair = lax.rem(z + Z_STEPS[j], 8) if layer == 0 else BLOCK_PAIRS[j]
             rows = hid_mm[k] if with_kept else hid_mm[k, 0:64]
-            y = jnp.dot(rows, wd[:, n * 256 : n * 256 + 256], preferred_element_type=F32)
+            cols = pl.ds(pl.multiple_of(pair * 256, 256), 256) if layer == 0 else slice(pair * 256, pair * 256 + 256)
+            y = jnp.dot(rows, wd[:, cols], preferred_element_type=F32)
             mine = jnp.where(core == 0, y[0:32], y[32:64])
             theirs = jnp.where(core == 0, y[32:64], y[0:32]).astype(BF)
             for m in range(2):
-                own[layer, k, 2 * n + m] = mine[:, m * 128 : m * 128 + 128]
-                sib_out[layer, k, 2 * n + m] = theirs[:, m * 128 : m * 128 + 128]
+                own[layer, k, 2 * j + m] = mine[:, m * 128 : m * 128 + 128]
+                sib_out[layer, k, 2 * j + m] = theirs[:, m * 128 : m * 128 + 128]
                 if with_kept:
-                    kp[2 * n + m] = y[64:72, m * 128 : m * 128 + 128]
+                    kp[2 * pair + m] = y[64:72, m * 128 : m * 128 + 128]
+            if j % 4 == 3 and not with_kept:
+                share_sums(layer, k, j // 4)
         if with_kept:
             kp_out[...] = kp[pl.ds(8 * other, 8)].astype(BF)
             remote(kp_out, kp_in, sending(kp_out), kp_sem.at[0], sibling).start()
-        sem = sending(sib_out.at[layer, k])
-        remote(sib_out.at[layer, k], sib_in.at[layer, k], sem, sib_sem.at[layer, k], sibling).start()
-
-    def scatter(layer, k):
-        arrived(sib_in.at[layer, k], sib_sem.at[layer, k])
-        sem = sending(sums_in.at[layer, k, pl.ds(1, NQ - 1)])
+            for half in range(2):
+                share_sums(layer, k, half)
+
+    def share_sums(layer, k, half):
+        at = pl.ds(8 * half, 8)
+        sem = sending(sib_out.at[layer, k, at])
+        remote(sib_out.at[layer, k, at], sib_in.at[layer, k, at], sem, sib_sem.at[layer, k, half], sibling).start()
+
+    def shared(layer, k, half):
+        arrived(sib_in.at[layer, k, pl.ds(8 * half, 8)], sib_sem.at[layer, k, half])
+
+    def scatter(k):
+        sem = sending(sums_in.at[k, pl.ds(1, NQ - 1)])
+        for j in range(8):
+            if j % 4 == 0:
+                shared(0, k, j // 4)
+            for dyh in (1, 0):
+                d = 2 * Z_STEPS[j] + dyh
+                if d == 0:
+                    continue
+                at = 2 * j + lax.rem(yh + dyh, 2)
+                sums[k, d] = (own[0, k, at] + sib_in[0, k, at].astype(F32)).astype(BF)
+                remote(sums.at[k, d], sums_in.at[k, d], sem, rsy_sem.at[k], to_chip(chip_at(d))).start()
+
+    def scatter_rows(layer, k):
+        for n in range(4):
+            if n % 2 == 0:
+                shared(layer, k, n // 2)
+            blocks = []
+            for m in range(4):
+                at = 2 * BLOCK_PAIRS.index((4 * m + n) // 2) + n % 2
+                blocks.append(own[layer, k, at] + sib_in[layer, k, at].astype(F32))
+            for g in range(4):
+                turned = turn([b[8 * g : 8 * g + 8] for b in blocks])
+                for a in range(4):
+                    last[layer - 1, k, 4 * g + a, :, n * 128 : n * 128 + 128] = turned[a].astype(BF)
+        sem = sending(last_in.at[layer - 1, k, pl.ds(1, NQ - 1)])
         for d in CHIP_STEPS:
             q = chip_at(d)
-            sums[layer, k, q] = (own[layer, k, q] + sib_in[layer, k, q].astype(F32)).astype(BF)
-            remote(sums.at[layer, k, q], sums_in.at[layer, k, d], sem, rsy_sem.at[layer, k], to_chip(q)).start()
-
-    def new_state(layer, k):
-        arrived(sums_in.at[layer, k, pl.ds(1, NQ - 1)], rsy_sem.at[layer, k])
-        total = own[layer, k, chip] + sib_in[layer, k, chip].astype(F32)
+            landing = last_in.at[layer - 1, k, d]
+            remote(last.at[layer - 1, k, q], landing, sem, last_sem.at[layer - 1, k], to_chip(q)).start()
+
+    quarter = lax.rem(chip, 4)
+
+    def own_rows(block):
+        turned = turn([block[:, m * 512 : m * 512 + 512] for m in range(4)])
+        rows = jnp.where(quarter == 0, turned[0], turned[1])
+        rows = jnp.where(quarter == 2, turned[2], rows)
+        return jnp.where(quarter == 3, turned[3], rows)
+
+    def add_sums(layer, k, rows):
+        arrived(last_in.at[layer - 1, k, pl.ds(1, NQ - 1)], last_sem.at[layer - 1, k])
+        total = last[layer - 1, k, chip].astype(F32)
         for d in range(1, NQ):
-            total = total + sums_in[layer, k, d].astype(F32)
-        return (x[layer, k, core, chip].astype(F32) + total).astype(BF).astype(F32)
+            total = total + last_in[layer - 1, k, d].astype(F32)
+        return (rows + total).astype(BF).astype(F32)
+
+    def write_rows(out, pair0, pair1):
+        even, odd = swap(pair0, pair1, 2)
+        out[:, 0:512] = even[0:4].astype(BF)
+        out[:, 512:1024] = odd[0:4].astype(BF)
+        out[:, 1024:1536] = even[4:8].astype(BF)
+        out[:, 1536:2048] = odd[4:8].astype(BF)
+
+    def new_state(k):
+        arrived(sums_in.at[k, pl.ds(1, NQ - 1)], rsy_sem.at[k])
+        total = own[0, k, 14 + yh] + sib_in[0, k, 14 + yh].astype(F32)
+        for d in range(1, NQ):
+            total = total + sums_in[k, d].astype(F32)
+        return (x[0, k, core, chip].astype(F32) + total).astype(BF).astype(F32)
 
     second_fwd = []
 
+    def take_tokens():
+        for d in CHIP_STEPS:
+            arrived(tok_in.at[chip_from(d)], tok_sem.at[d])
+        pair = lax.broadcasted_iota(jnp.int32, (8, 128), 0) // 2
+        for k in range(CHUNKS):
+            for g in range(4):
+                group = jnp.zeros((8, 128), F32)
+                for a in range(4):
+                    t = tok_in[4 * g + a].astype(F32)
+                    group = jnp.where(pair == a, t if a % 2 == k else pltpu.roll(t, 2, 0), group)
+                tokens[k, 8 * g : 8 * g + 8] = group
+
     def spread(k):
-        state = new_state(0, k)
-        if k == 0:
-            for d in CHIP_STEPS:
-                arrived(tok_in.at[chip_from(d)], tok_sem.at[d])
-        pair = lax.broadcasted_iota(jnp.int32, (8, 128), 0) // 2
-        groups = []
-        for g in range(4):
-            group = jnp.zeros((8, 128), F32)
-            for a in range(4):
-                t = tok_in[4 * g + a].astype(F32)
-                group = jnp.where(pair == a, t if a % 2 == k else pltpu.roll(t, 2, 0), group)
-            groups.append(group)
-        x[1, k, core, chip] = (state + jnp.concatenate(groups, axis=0)).astype(BF)
+        x[1, k, core, chip] = (new_state(k) + tokens[k]).astype(BF)
         piece = x.at[1, k, core, chip]
         sem = sending(x.at[1, k, 0, pl.ds(0, NQ - 1)])
         second_fwd.append(sending(x.at[1, k, 0]))
@@ -276,12 +335,13 @@
         up(0, k)
     for k in range(CHUNKS):
         act(0, k)
+    take_tokens()
     loads[8].wait()
     for k in range(CHUNKS):
         hidden(0, k)
         down(0, k)
     for k in range(CHUNKS):
-        scatter(0, k)
+        scatter(k)
     for k in range(CHUNKS):
         spread(k)
 
@@ -344,69 +404,30 @@
         up(2, k)
 
     for k in range(CHUNKS):
-        scatter(1, k)
+        scatter_rows(1, k)
     for k in range(CHUNKS):
         act(2, k)
-    for k in range(CHUNKS):
-        state = new_state(1, k).reshape(4, 8, 128)
-        dec_send[:, 8 * k : 8 * k + 8, :] = state.astype(BF)
-    sem = sending(dec_in.at[pl.ds(1, NQ - 1)])
-    for d in CHIP_STEPS:
-        q = chip_at(d)
-        remote(dec_send.at[q // 4], dec_in.at[d], sem, dec_sem.at[0], to_chip(q)).start()
-    dec_in[0] = dec_send[chip // 4]
-
     for k in range(CHUNKS):
         hidden(2, k)
         down(2, k)
     for k in range(CHUNKS):
-        arrived(sib_in.at[2, k], sib_sem.at[2, k])
-        for n in range(4):
-            blocks = [own[2, k, 4 * m + n] + sib_in[2, k, 4 * m + n].astype(F32) for m in range(4)]
-            for g in range(4):
-                turned = turn([b[8 * g : 8 * g + 8] for b in blocks])
-                for a in range(4):
-                    last[k, 4 * g + a, :, n * 128 : n * 128 + 128] = turned[a].astype(BF)
-        sem = sending(last_in.at[k, pl.ds(1, NQ - 1)])
-        for d in CHIP_STEPS:
-            q = chip_at(d)
-            remote(last.at[k, q], last_in.at[k, d], sem, last_sem.at[k], to_chip(q)).start()
-
-    arrived(dec_in.at[pl.ds(1, NQ - 1)], dec_sem.at[0])
-    quarter = lax.rem(chip, 4)
-
-    def own_pair(block):
-        block = jnp.where(quarter >= 2, pltpu.roll(block, 4, 0), block)
-        return jnp.where(lax.rem(quarter, 2) == 1, pltpu.roll(block, 6, 0), block)
-
-    for cb in range(NQ):
-        step = lax.rem(z + 8 - cb // 2, 8) * 2 + lax.rem(yh + cb % 2, 2)
-        both = dec_in[step].astype(F32)
-        low, high = own_pair(both[0:8]), pltpu.roll(own_pair(both[8:16]), 2, 0)
-        rows = jnp.where(lax.broadcasted_iota(jnp.int32, (8, 128), 0) < 2, low, high)
-        dec_out[:, cb * 128 : cb * 128 + 128] = rows[0:4].astype(BF)
-
+        scatter_rows(2, k)
+
+    group = chip // 4
     results = []
     for k in range(CHUNKS):
-        mine = rows_f[k, core, chip // 4]
-        turned = turn([mine[:, m * 512 : m * 512 + 512] for m in range(4)])
-        total = jnp.where(quarter == 0, turned[0], turned[1])
-        total = jnp.where(quarter == 2, turned[2], total)
-        total = jnp.where(quarter == 3, turned[3], total)
-        results.append(total)
+        columns = []
+        for cb in range(NQ):
+            rows = x[1, k, core, cb].astype(F32)
+            eight = jnp.where(group == 0, rows[0:8], rows[8:16])
+            eight = jnp.where(group == 2, rows[16:24], eight)
+            columns.append(jnp.where(group == 3, rows[24:32], eight))
+        results.append(add_sums(1, k, own_rows(jnp.concatenate(columns, axis=1))))
+    write_rows(dec_out, *results)
+    residuals = [own_rows(rows_f[k, core, group]) for k in range(CHUNKS)]
     for i, ref in enumerate(sent):
         remote(ref, ref, snd.at[i], snd.at[i], sibling).wait_send()
-    for k in range(CHUNKS):
-        arrived(last_in.at[k, pl.ds(1, NQ - 1)], last_sem.at[k])
-        total = last[k, chip].astype(F32)
-        for d in range(1, NQ):
-            total = total + last_in[k, d].astype(F32)
-        results[k] = (results[k] + total).astype(BF).astype(F32)
-    even, odd = swap(results[0], results[1], 2)
-    ev_out[:, 0:512] = even[0:4].astype(BF)
-    ev_out[:, 512:1024] = odd[0:4].astype(BF)
-    ev_out[:, 1024:1536] = even[4:8].astype(BF)
-    ev_out[:, 1536:2048] = odd[4:8].astype(BF)
+    write_rows(ev_out, *[add_sums(2, k, residuals[k]) for k in range(CHUNKS)])
 
 
 def on_device(
@@ -427,16 +448,16 @@
         V((*LK, 8, 8, HID), BF), V((CHUNKS, 80, HID), BF),
         V((*LK, NQ, 32, 128), F32),
         V((*LK, NQ, 32, 128), BF), V((*LK, NQ, 32, 128), BF),
-        V((2, CHUNKS, NQ, 32, 128), BF), V((2, CHUNKS, NQ, 32, 128), BF),
+        V((CHUNKS, NQ, 32, 128), BF), V((CHUNKS, NQ, 32, 128), BF),
         V((NQ, 8, 128), BF), V((NQ, 8, 128), BF),
         V((NQ, 8, 128), F32), V((8, 8, 128), BF), V((8, 8, 128), BF),
         V((8, 8, 128), BF), V((NQ, 8, 8, 128), BF), V((NQ, 8, 128), BF),
         V((CHUNKS, 2, 4, 8, WIDTH), F32),
-        V((4, 16, 128), BF), V((NQ, 16, 128), BF),
-        V((CHUNKS, NQ, 8, 512), BF), V((CHUNKS, NQ, 8, 512), BF),
+        V((CHUNKS, 32, 128), F32),
+        V((2, CHUNKS, NQ, 8, 512), BF), V((2, CHUNKS, NQ, 8, 512), BF),
         dma((9,)), dma((48,)), dma((CHUNKS, NQ)), dma((CHUNKS,)), dma((NQ,)),
         dma((CHUNKS, NQ)), dma((CHUNKS,)), dma(LK), dma((*LK, 8)),
-        dma(LK), dma(LK), dma((1,)), dma((1,)), dma((1,)), dma((1,)), dma((CHUNKS,)),
+        dma((*LK, 2)), dma((CHUNKS,)), dma((1,)), dma((1,)), dma((1,)), dma((2, CHUNKS)),
     ]
     return pl.pallas_call(
         kernel,

time: 106 us -> 106 us (level)
  no operation moved by 1% of the time
where the time goes in v4:
time: 106 us; the launch traced here: 105 us
  Pallas kernels  102 us (96%)
  local copies, waits for them, and re-layouts  2.66 us (3%)
    pallas_call x1, Pallas kernels, on_device(): pl.pallas_call(kernel, out_shape=(jax.ShapeDtypeStruct((4, WIDTH), BF), j...  102 us
    unnamed x2, local copies, waits for them, and re-layouts  2.66 us

profile of v4, /device:TPU:1, one launch (start us, length us, event | category | flops | bytes accessed | tf_op | source)
XLA Modules:
  0.0 105.3 jit_solution(3225235871080007439)
XLA Ops:
  0.6 102.0 %beam_steps.1 = (bf16[4,2048]{1,0:T(4,128)(2,1)}, bf16[4,2048]{1,0:T(4,128)(2,1)}) custom-call(bf16[4,2048]{1,0:T(4,128)(2,1)} %beam_hbm.1, bf16[2,4,2048]{2,1,0:T(4,128)(2,1)} %tok_hbm.1, bf16[2048]{0:T(1024)(128)(2,1)} %gain_hbm.1, s32[8]{0:T(128)} %kept_hbm.1, s32[8,16]{1,0:T(8,128)} %ids_hbm.1, bf16[2048,896]{1,0:T(8,128)(2,1)} %wg_hbm.1, ...), custom_call_target="tpu_custom_call" | custom-call | tf_op jit(solution)/shard_map/beam_steps/pallas_call | solution.py:462
  102.7 1.3 %copy.13 = bf16[4,2048]{1,0:T(4,128)(2,1)} copy(bf16[4,2048]{1,0:T(4,128)(2,1)} %get-tuple-element.4) | data formatting | bytes 32768
  104.0 1.3 %copy.14 = bf16[4,2048]{1,0:T(4,128)(2,1)} copy(bf16[4,2048]{1,0:T(4,128)(2,1)} %get-tuple-element.5) | data formatting | bytes 32768

commit v5 on v4

--- a/solution.py
+++ b/solution.py
@@ -18,7 +18,8 @@
 CHIP_STEPS = sorted(range(1, NQ), key=lambda d: -(min(d // 2, 8 - d // 2) + 2 * (d % 2)))
 Z_STEPS = (4, 3, 5, 2, 6, 1, 7, 0)
 BLOCK_PAIRS = (0, 2, 4, 6, 1, 3, 5, 7)
-GX_STEPS = sorted(range(1, 8), key=lambda e: -(min(e % 4, 4 - e % 4) + e // 4))
+GX_STEPS = sorted(range(1, 8), key=lambda e: (-min(e % 4, 4 - e % 4), -(e // 4)))
+NEAR_FIRST = CHIP_STEPS[::-1]
 
 
 def swap(a, b, rows):
@@ -37,9 +38,9 @@
     dec_out, ev_out,
     beam, tok, gain, kept, ids, wg, wu, wd, tab, words, first, x, xs, part, part_in, hid, hid_mm,
     own, sib_out, sib_in, sums, sums_in, tok_out, tok_in,
-    kp, kp_out, kp_in, ks, ks_in, pick_all, rows_f, tokens, last, last_in,
+    kp, kp_out, kp_in, ks, ks_in, pick_all, rows_f, tokens, last, last_in, z_in, joined, pair_out, pair_in,
     load_sem, snd, first_sem, first_fwd, tok_sem, ag_sem, ag_fwd, rsx_sem, agx_sem,
-    sib_sem, rsy_sem, kp_sem, ks_sem, pick_sem, last_sem,
+    sib_sem, rsy_sem, kp_sem, ks_sem, pick_sem, last_sem, z_sem, pair_sem,
 ):
     gx, gy = lax.axis_index("gx"), lax.axis_index("gy")
     px, pyl = lax.rem(gx, NX), gx // NX
@@ -249,11 +250,31 @@
                 turned = turn([b[8 * g : 8 * g + 8] for b in blocks])
                 for a in range(4):
                     last[layer - 1, k, 4 * g + a, :, n * 128 : n * 128 + 128] = turned[a].astype(BF)
-        sem = sending(last_in.at[layer - 1, k, pl.ds(1, NQ - 1)])
+        if layer == 1:
+            sem = sending(z_in.at[k, pl.ds(1, 7)])
+            for dz in Z_STEPS[:7]:
+                zt = lax.rem(z + dz, 8)
+                piece = last.at[0, k, pl.ds(2 * zt, 2)]
+                remote(piece, z_in.at[k, dz], sem, z_sem.at[k], to_chip(2 * zt + yh)).start()
+            return
+        sem = sending(last_in.at[k, pl.ds(1, NQ - 1)])
         for d in CHIP_STEPS:
             q = chip_at(d)
-            landing = last_in.at[layer - 1, k, d]
-            remote(last.at[layer - 1, k, q], landing, sem, last_sem.at[layer - 1, k], to_chip(q)).start()
+            remote(last.at[1, k, q], last_in.at[k, d], sem, last_sem.at[k], to_chip(q)).start()
+
+    def join_pairs(k):
+        arrived(z_in.at[k, pl.ds(1, 7)], z_sem.at[k])
+        for mine in range(2):
+            at = yh if mine else 1 - yh
+            total = last[0, k, 2 * z + at].astype(F32)
+            for dz in range(1, 8):
+                total = total + z_in[k, dz, at].astype(F32)
+            if mine:
+                joined[k] = total
+            else:
+                pair_out[k] = total.astype(BF)
+                partner = to_chip(2 * z + 1 - yh)
+                remote(pair_out.at[k], pair_in.at[k], sending(pair_out.at[k]), pair_sem.at[k], partner).start()
 
     quarter = lax.rem(chip, 4)
 
@@ -264,10 +285,14 @@
         return jnp.where(quarter == 3, turned[3], rows)
 
     def add_sums(layer, k, rows):
-        arrived(last_in.at[layer - 1, k, pl.ds(1, NQ - 1)], last_sem.at[layer - 1, k])
-        total = last[layer - 1, k, chip].astype(F32)
-        for d in range(1, NQ):
-            total = total + last_in[layer - 1, k, d].astype(F32)
+        if layer == 1:
+            arrived(pair_in.at[k], pair_sem.at[k])
+            total = joined[k] + pair_in[k].astype(F32)
+        else:
+            arrived(last_in.at[k, pl.ds(1, NQ - 1)], last_sem.at[k])
+            total = last[1, k, chip].astype(F32)
+            for d in range(1, NQ):
+                total = total + last_in[k, d].astype(F32)
         return (rows + total).astype(BF).astype(F32)
 
     def write_rows(out, pair0, pair1):
@@ -307,18 +332,22 @@
             remote(piece, piece, sem, ag_sem.at[k, d], to_chip(chip_at(d))).start()
         remote(piece, piece, second_fwd[k], ag_fwd.at[k], sibling).start()
 
-    def collect(k):
-        for d in reversed(CHIP_STEPS):
+    def pass_on(k, steps):
+        for d in steps:
             piece = x.at[1, k, core, chip_from(d)]
             arrived(piece, ag_sem.at[k, d])
             remote(piece, piece, second_fwd[k], ag_fwd.at[k], sibling).start()
-        arrived(x.at[1, k, other], ag_fwd.at[k])
-
-    for k in range(CHUNKS):
-        for d in reversed(CHIP_STEPS):
+
+    def pass_on_first(k, steps):
+        for d in steps:
             piece = first.at[k, core, chip_from(d)]
             arrived(piece, first_sem.at[k, d])
             remote(piece, piece, forward[k], first_fwd.at[k], sibling).start()
+
+    pass_on_first(0, NEAR_FIRST)
+    for k in range(CHUNKS):
+        if k == 1:
+            pass_on_first(1, NEAR_FIRST)
         arrived(first.at[k, other], first_fwd.at[k])
         for h in range(2):
             for g in range(4):
@@ -330,6 +359,7 @@
                 x[0, k, h, cb] = block.reshape(32, 128).astype(BF)
         prepare(0, k)
         if k == 0:
+            pass
             loads[6].wait()
             loads[7].wait()
         up(0, k)
@@ -340,14 +370,18 @@
     for k in range(CHUNKS):
         hidden(0, k)
         down(0, k)
-    for k in range(CHUNKS):
         scatter(k)
     for k in range(CHUNKS):
         spread(k)
 
-    for k in range(CHUNKS):
-        collect(k)
+    pass_on(0, NEAR_FIRST)
+    for k in range(CHUNKS):
+        if k == 1:
+            pass_on(1, NEAR_FIRST)
+        arrived(x.at[1, k, other], ag_fwd.at[k])
         prepare(1, k)
+        if k == 0:
+            pass
         up(1, k)
     for k in range(CHUNKS):
         act(1, k)
@@ -358,6 +392,8 @@
         kept_mixed.append(jnp.dot(picker, column, preferred_element_type=F32)[0:8])
     for k in range(CHUNKS):
         hidden(1, k)
+        if k == 0:
+            down(1, 0)
 
     def pick_hidden(n, carry):
         cols = pl.ds(pl.multiple_of(n * 128, 128), 128)
@@ -370,7 +406,6 @@
 
     lax.fori_loop(0, HID // 128, pick_hidden, 0)
     down(1, 1, True)
-    down(1, 0)
 
     arrived(kp_in, kp_sem.at[0])
     ks[...] = (kp[pl.ds(8 * core, 8)] + kp_in[...].astype(F32)).astype(BF)
@@ -408,9 +443,10 @@
     for k in range(CHUNKS):
         act(2, k)
     for k in range(CHUNKS):
+        join_pairs(k)
+    for k in range(CHUNKS):
         hidden(2, k)
         down(2, k)
-    for k in range(CHUNKS):
         scatter_rows(2, k)
 
     group = chip // 4
@@ -454,10 +490,12 @@
         V((8, 8, 128), BF), V((NQ, 8, 8, 128), BF), V((NQ, 8, 128), BF),
         V((CHUNKS, 2, 4, 8, WIDTH), F32),
         V((CHUNKS, 32, 128), F32),
-        V((2, CHUNKS, NQ, 8, 512), BF), V((2, CHUNKS, NQ, 8, 512), BF),
+        V((2, CHUNKS, NQ, 8, 512), BF), V((CHUNKS, NQ, 8, 512), BF),
+        V((CHUNKS, 8, 2, 8, 512), BF), V((CHUNKS, 8, 512), F32),
+        V((CHUNKS, 8, 512), BF), V((CHUNKS, 8, 512), BF),
         dma((9,)), dma((48,)), dma((CHUNKS, NQ)), dma((CHUNKS,)), dma((NQ,)),
         dma((CHUNKS, NQ)), dma((CHUNKS,)), dma(LK), dma((*LK, 8)),
-        dma((*LK, 2)), dma((CHUNKS,)), dma((1,)), dma((1,)), dma((1,)), dma((2, CHUNKS)),
+        dma((*LK, 2)), dma((CHUNKS,)), dma((1,)), dma((1,)), dma((1,)), dma((CHUNKS,)), dma((CHUNKS,)), dma((CHUNKS,)),
     ]
     return pl.pallas_call(
         kernel,

time: 106 us -> 100 us (0.943)
  Pallas kernels: 102 us -> 96.4 us
    pallas_call x1, Pallas kernels: 102 us -> 96.4 us  [on_device(): pl.pallas_call(kernel, out_shape=(jax.ShapeDtypeStruct((4, WIDTH), BF), j...]
where the time goes in v5:
time: 100 us; the launch traced here: 99.7 us
  Pallas kernels  96.4 us (96%)
  local copies, waits for them, and re-layouts  2.66 us (3%)
    pallas_call x1, Pallas kernels, on_device(): pl.pallas_call(kernel, out_shape=(jax.ShapeDtypeStruct((4, WIDTH), BF), j...  96.4 us
    unnamed x2, local copies, waits for them, and re-layouts  2.66 us

profile of v5, /device:TPU:1, one launch (start us, length us, event | category | flops | bytes accessed | tf_op | source)
XLA Modules:
  0.0 99.7 jit_solution(7687097594626571871)
XLA Ops:
  0.6 96.4 %beam_steps.1 = (bf16[4,2048]{1,0:T(4,128)(2,1)}, bf16[4,2048]{1,0:T(4,128)(2,1)}) custom-call(bf16[4,2048]{1,0:T(4,128)(2,1)} %beam_hbm.1, bf16[2,4,2048]{2,1,0:T(4,128)(2,1)} %tok_hbm.1, bf16[2048]{0:T(1024)(128)(2,1)} %gain_hbm.1, s32[8]{0:T(128)} %kept_hbm.1, s32[8,16]{1,0:T(8,128)} %ids_hbm.1, bf16[2048,896]{1,0:T(8,128)(2,1)} %wg_hbm.1, ...), custom_call_target="tpu_custom_call" | custom-call | tf_op jit(solution)/shard_map/beam_steps/pallas_call | solution.py:500
  97.1 1.3 %copy.13 = bf16[4,2048]{1,0:T(4,128)(2,1)} copy(bf16[4,2048]{1,0:T(4,128)(2,1)} %get-tuple-element.4) | data formatting | bytes 32768
  98.4 1.3 %copy.14 = bf16[4,2048]{1,0:T(4,128)(2,1)} copy(bf16[4,2048]{1,0:T(4,128)(2,1)} %get-tuple-element.5) | data formatting | bytes 32768

commit v6 on v5

--- a/solution.py
+++ b/solution.py
@@ -35,8 +35,8 @@
 
 def kernel(
     beam_hbm, tok_hbm, gain_hbm, kept_hbm, ids_hbm, wg_hbm, wu_hbm, wd_hbm, tab_hbm,
-    dec_out, ev_out,
-    beam, tok, gain, kept, ids, wg, wu, wd, tab, words, first, x, xs, part, part_in, hid, hid_mm,
+    out,
+    beam, tok, gain, kept, ids, wg, wu, wd, tab, words, first, x, xs, xs_all, part, part_in, hid, hid_mm,
     own, sib_out, sib_in, sums, sums_in, tok_out, tok_in,
     kp, kp_out, kp_in, ks, ks_in, pick_all, rows_f, tokens, last, last_in, z_in, joined, pair_out, pair_in,
     load_sem, snd, first_sem, first_fwd, tok_sem, ag_sem, ag_fwd, rsx_sem, agx_sem,
@@ -148,7 +148,7 @@
     picker = (kept_rows == row_of((16, 128), 1)).astype(F32).astype(BF)
 
     def prepare(layer, k):
-        squares = []
+        totals = []
         for h in range(2):
             total = jnp.zeros((32, 128), F32)
             for cb in range(NQ):
@@ -156,7 +156,11 @@
                 total = total + v * v
                 cols = slice(cb * 128, cb * 128 + 128)
                 xs[h * 32 : h * 32 + 32, cols] = (v * gain[cols].astype(F32)[None, :]).astype(BF)
-            squares.append(jnp.sum(total, axis=1, keepdims=True))
+            totals.append(total)
+        put_squares(layer, k, totals)
+
+    def put_squares(layer, k, totals):
+        squares = [jnp.sum(total, axis=1, keepdims=True) for total in totals]
         whole = jnp.broadcast_to(jnp.concatenate(squares, axis=0), (64, 128))
         high = whole.astype(BF).astype(F32)
         both = jnp.concatenate([high.reshape(8, 8, 128), (whole - high).reshape(8, 8, 128)], axis=1)
@@ -169,6 +173,9 @@
             y = jnp.dot(xs[...], weights, preferred_element_type=F32)
             both = jnp.concatenate([y[:, :128].reshape(8, 8, 128), y[:, 128:].reshape(8, 8, 128)], axis=1)
             part[layer, k, :, :, cols] = both.astype(BF)
+        send_parts(layer, k)
+
+    def send_parts(layer, k):
         sem = sending(part_in.at[layer, k, pl.ds(1, 7)])
         for e in GX_STEPS:
             p = gx_at(e)
@@ -424,6 +431,7 @@
 
     upper = lax.broadcasted_iota(jnp.int32, (8, 128), 0) < 4
     for k in range(CHUNKS):
+        totals = [jnp.zeros((32, 128), F32) for h in range(2)]
         for cb in range(NQ):
             cols = slice(cb * 128, cb * 128 + 128)
             chosen = pick_all[cb].astype(F32)
@@ -432,11 +440,21 @@
             )
             for h in range(2):
                 at = 64 * k + 32 * h
-                rows = (chosen + words[at : at + 32, cols].astype(F32)).astype(BF)
-                x[2, k, h, cb] = rows
-                rows_f[k, h, :, :, cols] = rows.astype(F32).reshape(4, 8, 128)
-        prepare(2, k)
-        up(2, k)
+                rows = (chosen + words[at : at + 32, cols].astype(F32)).astype(BF).astype(F32)
+                rows_f[k, h, :, :, cols] = rows.reshape(4, 8, 128)
+                totals[h] = totals[h] + rows * rows
+                xs_all[at : at + 32, cols] = (rows * gain[cols].astype(F32)[None, :]).astype(BF)
+        put_squares(2, k, totals)
+    for n in range(HID // 128):
+        cols = slice(n * 128, n * 128 + 128)
+        weights = jnp.concatenate([wg[:, cols], wu[:, cols]], axis=1)
+        y = jnp.dot(xs_all[...], weights, preferred_element_type=F32)
+        for k in range(CHUNKS):
+            rows = y[64 * k : 64 * k + 64]
+            both = jnp.concatenate([rows[:, :128].reshape(8, 8, 128), rows[:, 128:].reshape(8, 8, 128)], axis=1)
+            part[2, k, :, :, cols] = both.astype(BF)
+    for k in range(CHUNKS):
+        send_parts(2, k)
 
     for k in range(CHUNKS):
         scatter_rows(1, k)
@@ -459,11 +477,11 @@
             eight = jnp.where(group == 2, rows[16:24], eight)
             columns.append(jnp.where(group == 3, rows[24:32], eight))
         results.append(add_sums(1, k, own_rows(jnp.concatenate(columns, axis=1))))
-    write_rows(dec_out, *results)
+    write_rows(out.at[0], *results)
     residuals = [own_rows(rows_f[k, core, group]) for k in range(CHUNKS)]
     for i, ref in enumerate(sent):
         remote(ref, ref, snd.at[i], snd.at[i], sibling).wait_send()
-    write_rows(ev_out, *[add_sums(2, k, residuals[k]) for k in range(CHUNKS)])
+    write_rows(out.at[1], *[add_sums(2, k, residuals[k]) for k in range(CHUNKS)])
 
 
 def on_device(
@@ -478,8 +496,8 @@
         V((WIDTH, HID), BF), V((WIDTH, HID), BF), V((HID, WIDTH), BF), V((256, WIDTH), BF),
         V((128, WIDTH), BF),
         V((CHUNKS, 2, NQ, 8, 512), BF),
-        V((*LK, 2, NQ, 32, 128), BF),
-        V((64, WIDTH), BF),
+        V((2, CHUNKS, 2, NQ, 32, 128), BF),
+        V((64, WIDTH), BF), V((128, WIDTH), BF),
         V((*LK, 8, 16, 1024), BF), V((*LK, 8, 16, 1024), BF),
         V((*LK, 8, 8, HID), BF), V((CHUNKS, 80, HID), BF),
         V((*LK, NQ, 32, 128), F32),
@@ -497,11 +515,11 @@
         dma((CHUNKS, NQ)), dma((CHUNKS,)), dma(LK), dma((*LK, 8)),
         dma((*LK, 2)), dma((CHUNKS,)), dma((1,)), dma((1,)), dma((1,)), dma((CHUNKS,)), dma((CHUNKS,)), dma((CHUNKS,)),
     ]
-    return pl.pallas_call(
+    both = pl.pallas_call(
         kernel,
-        out_shape=(jax.ShapeDtypeStruct((4, WIDTH), BF), jax.ShapeDtypeStruct((4, WIDTH), BF)),
+        out_shape=jax.ShapeDtypeStruct((2, 4, WIDTH), BF),
         in_specs=[hbm] * 9,
-        out_specs=(vmem, vmem),
+        out_specs=vmem,
         scratch_shapes=scratch,
         compiler_params=pltpu.CompilerParams(
             collective_id=0, has_side_effects=True, vmem_limit_bytes=56 * 2**20
@@ -511,6 +529,7 @@
         beam_states, step_tokens, norm_gain, kept_beams, prompt_ids,
         w_gate, w_up, w_down, prompt_table,
     )
+    return both[0], both[1]
 
 
 def solution(mesh):

time: 100 us -> 98.3 us (0.983)
  local copies, waits for them, and re-layouts: 2.66 us -> 1.36 us
    unnamed x2 -> x0, local copies, waits for them, and re-layouts: 2.66 us -> none
    squeeze x0 -> x1, local copies, waits for them, and re-layouts: none -> 1.36 us  [on_device(): return (both[0], both[1])]
where the time goes in v6:
time: 98.3 us; the launch traced here: 98 us
  Pallas kernels  96 us (98%)
  local copies, waits for them, and re-layouts  1.36 us (1%)
    pallas_call x1, Pallas kernels, on_device(): pl.pallas_call(kernel, out_shape=jax.ShapeDtypeStruct((2, 4, WIDTH), BF),...  96 us

profile of v6, /device:TPU:1, one launch (start us, length us, event | category | flops | bytes accessed | tf_op | source)
XLA Modules:
  0.0 98.0 jit_solution(14636470828674164418)
XLA Ops:
  0.6 96.0 %beam_steps.1 = bf16[2,4,2048]{2,1,0:T(4,128)(2,1)} custom-call(bf16[4,2048]{1,0:T(4,128)(2,1)} %beam_hbm.1, bf16[2,4,2048]{2,1,0:T(4,128)(2,1)} %tok_hbm.1, bf16[2048]{0:T(1024)(128)(2,1)} %gain_hbm.1, s32[8]{0:T(128)} %kept_hbm.1, s32[8,16]{1,0:T(8,128)} %ids_hbm.1, bf16[2048,896]{1,0:T(8,128)(2,1)} %wg_hbm.1, bf16[2048,896]{1,0:T(8,128)(2,1)} %wu_hbm.1, ...), custom_call_target="tpu_custom_call" | custom-call | tf_op jit(solution)/shard_map/beam_steps/pallas_call | solution.py:518
  96.6 1.4 %slice_bitcast_fusion = (bf16[4,2048]{1,0:T(4,128)(2,1)}, bf16[4,2048]{1,0:T(4,128)(2,1)}) fusion(bf16[2,4,2048]{2,1,0:T(4,128)(2,1)} %beam_steps.1), kind=kLoop, calls=%fused_computation | loop fusion | bytes 65536 | tf_op jit(solution)/shard_map/squeeze | solution.py:532

commit v7 on v6

--- a/solution.py
+++ b/solution.py
@@ -15,7 +15,7 @@
 LAYERS, CHUNKS = 3, 2
 MESH = pl.DeviceIdType.MESH
 
-CHIP_STEPS = sorted(range(1, NQ), key=lambda d: -(min(d // 2, 8 - d // 2) + 2 * (d % 2)))
+CHIP_STEPS = sorted(range(1, NQ), key=lambda d: (-(d % 2), -min(d // 2, 8 - d // 2)))
 Z_STEPS = (4, 3, 5, 2, 6, 1, 7, 0)
 BLOCK_PAIRS = (0, 2, 4, 6, 1, 3, 5, 7)
 GX_STEPS = sorted(range(1, 8), key=lambda e: (-min(e % 4, 4 - e % 4), -(e // 4)))

time: 98.3 us -> 98 us (level)
  no operation moved by 1% of the time
where the time goes in v7:
time: 98 us; the launch traced here: 97.7 us
  Pallas kernels  95.7 us (98%)
  local copies, waits for them, and re-layouts  1.36 us (1%)
    pallas_call x1, Pallas kernels, on_device(): pl.pallas_call(kernel, out_shape=jax.ShapeDtypeStruct((2, 4, WIDTH), BF),...  95.7 us

profile of v7, /device:TPU:1, one launch (start us, length us, event | category | flops | bytes accessed | tf_op | source)
XLA Modules:
  0.0 97.7 jit_solution(7805769811543354986)
XLA Ops:
  0.6 95.7 %beam_steps.1 = bf16[2,4,2048]{2,1,0:T(4,128)(2,1)} custom-call(bf16[4,2048]{1,0:T(4,128)(2,1)} %beam_hbm.1, bf16[2,4,2048]{2,1,0:T(4,128)(2,1)} %tok_hbm.1, bf16[2048]{0:T(1024)(128)(2,1)} %gain_hbm.1, s32[8]{0:T(128)} %kept_hbm.1, s32[8,16]{1,0:T(8,128)} %ids_hbm.1, bf16[2048,896]{1,0:T(8,128)(2,1)} %wg_hbm.1, bf16[2048,896]{1,0:T(8,128)(2,1)} %wu_hbm.1, ...), custom_call_target="tpu_custom_call" | custom-call | tf_op jit(solution)/shard_map/beam_steps/pallas_call | solution.py:518
  96.3 1.4 %slice_bitcast_fusion = (bf16[4,2048]{1,0:T(4,128)(2,1)}, bf16[4,2048]{1,0:T(4,128)(2,1)}) fusion(bf16[2,4,2048]{2,1,0:T(4,128)(2,1)} %beam_steps.1), kind=kLoop, calls=%fused_computation | loop fusion | bytes 65536 | tf_op jit(solution)/shard_map/squeeze | solution.py:532
